TPU v7x, 256 devices: a whole 4x4x8 slice. The times are simulated.
256 devices in a mesh: grid: 32 (over z, x), layer: 8 (over y, core).
Axes of the slice: x: 4, y: 4, z: 8, core: 2. Of those that a mesh axis runs over, the one named last changes fastest.
Arguments:
- a_tiles: bfloat16 [1536, 16, 128, 128], P('grid', 'layer'), may hold values from -0.5 to 0.5
- a_cols: int32 [1536, 16], P('grid', 'layer'), may hold values from 0 to 1535, as said below
- p_tiles: bfloat16 [1536, 2, 128, 128], P('grid'), may hold values from -0.5 to 0.5
- p_cols: int32 [1536, 2], P('grid'), may hold values from 0 to 31, as said below
Outputs:
- coarse: bfloat16 [32, 32, 128, 128], P('grid', 'layer')
Inputs may be any that keep to these rules, and one draw needn't show every extreme that they name: `a_cols`: tile j of A lies in fine tile row j, held by grid index j // 48. Of the 48 x 2 tiles of one device, at most 6 tiles have their column on any one grid index, and exactly 6 on the device's own grid index. `p_cols`: fine tile row i, with g = i // 48, names 2 distinct coarse columns out of g - 1, g, g + 1 taken modulo 32.
All inputs are finite; a program needn't handle non-finite values.
Results may differ from a plain program's by a relative error of at most 0.0049.
Values may be sent and summed in bfloat16 or wider, within the bound.
A program may use at most 128 MiB of HBM per device.

v0:
```python
import jax
import jax.numpy as jnp
from jax import lax
from jax.sharding import PartitionSpec as P


def with_halo(cells, sides, width):
    for axis, dim in sides:
        count = lax.axis_size(axis)
        head = lax.slice_in_dim(cells, 0, width, axis=dim)
        tail = lax.slice_in_dim(cells, cells.shape[dim] - width, cells.shape[dim], axis=dim)
        cells = jnp.concatenate(
            [
                lax.ppermute(tail, axis, [(i, (i + 1) % count) for i in range(count)]),
                cells,
                lax.ppermute(head, axis, [((i + 1) % count, i) for i in range(count)]),
            ],
            axis=dim,
        )
    return cells


def local(a_tiles, a_cols, p_tiles, p_cols):
    fine_rows, per_layer, tile_size, unused = a_tiles.shape
    p_width = p_tiles.shape[1]
    grid_count = lax.axis_size("grid")
    slot_total = fine_rows * per_layer
    capacity = 2 * slot_total // grid_count
    grid_index = lax.axis_index("grid")
    flat_cols = a_cols.reshape(slot_total)
    owners = flat_cols // fine_rows
    local_rows = flat_cols % fine_rows
    owner_hits = (owners[:, None] == jnp.arange(grid_count, dtype=jnp.int32)[None, :]).astype(
        jnp.int32
    )
    position = jnp.sum((jnp.cumsum(owner_hits, axis=0) - owner_hits) * owner_hits, axis=1)
    slot_index = owners * capacity + position
    requests = jnp.zeros((grid_count * capacity,), jnp.int32).at[slot_index].set(local_rows)
    requests = requests.reshape(grid_count, capacity)
    a_flat = a_tiles.reshape(slot_total, tile_size, tile_size)
    wanted = lax.all_to_all(requests, "grid", split_axis=0, concat_axis=0, tiled=True)
    returned, returned_cols = (
        lax.all_to_all(p_tiles[wanted], "grid", split_axis=0, concat_axis=0, tiled=True),
        lax.all_to_all(p_cols[wanted], "grid", split_axis=0, concat_axis=0, tiled=True),
    )
    fetched = returned.reshape(grid_count * capacity, p_width, tile_size, tile_size)[slot_index]
    coarse_cols = returned_cols.reshape(grid_count * capacity, p_width)[slot_index]
    products = jnp.einsum(
        "nab,ntbc->ntac", a_flat, fetched, preferred_element_type=jnp.float32
    ).astype(jnp.bfloat16)
    products = products.reshape(fine_rows, per_layer, p_width, tile_size, tile_size)
    triple = jnp.einsum("rsba,rktbc->rkstac", p_tiles, products, preferred_element_type=jnp.float32)
    band_index = (p_cols - grid_index + 1) % grid_count
    targets = band_index[:, None, :, None] * grid_count + coarse_cols.reshape(
        fine_rows, per_layer, 1, p_width
    )
    targets = targets.reshape(-1)
    partials = jnp.zeros((3 * grid_count, tile_size * tile_size), jnp.float32)
    partials = partials.at[targets].add(triple.reshape(targets.shape[0], tile_size * tile_size))
    partials = partials.reshape(3, grid_count, tile_size, tile_size)
    with_rims = with_halo(partials, (("grid", 0),), 1)
    owned_sum = lax.psum_scatter(
        with_rims[2] + with_rims[0] + with_rims[4], "layer", scatter_dimension=0, tiled=True
    )
    return owned_sum.astype(jnp.bfloat16)[None]


def solution(mesh):
    return jax.shard_map(
        local,
        mesh=mesh,
        in_specs=(
            P("grid", "layer", None, None),
            P("grid", "layer"),
            P("grid", None, None, None),
            P("grid", None),
        ),
        out_specs=P("grid", "layer", None, None),
        check_vma=False,
    )
```

profile of v0, /device:TPU:1, one launch (start us, length us, event | category | flops | bytes accessed | tf_op | source)
XLA Modules:
  0.0 588.4 jit_solution(6878521383165087173)
XLA Ops:
  6.5 0.8 compare_and_fusion
  7.4 0.8 broadcast_remainder_fusion
  8.2 0.1 copy.25
  8.3 0.1 div.24
  8.4 0.1 div.23
  8.5 0.1 copy.24
  8.6 0.1 and.31
  8.8 0.1 copy.26
  8.9 0.1 ne.60
  9.1 0.1 rem.58
  9.3 0.1 reduce_window_sum.11
  9.5 0.2 select_reduce_fusion
  9.7 0.9 scatter_custom_fusion
  10.6 0.7 all_to_all.14
  11.3 11.9 %all-to-all-start = ((s32[32,1,6]{2,1,0:T(1,128)}), s32[32,1,6]{2,1,0:T(1,128)S(1)}, u32[]{:S(2)}, u32[]{:S(2)}) async-start(s32[32,1,6]{2,1,0:T(1,128)} %bitcast.2), calls=%async_computation | async-start | bytes 32768 | tf_op jit(solution)/shard_map/all_to_all | solution.py:41
  23.1 0.8 copy.30
  23.9 7.7 %all-to-all-done = s32[32,1,6]{2,1,0:T(1,128)S(1)} async-done(((s32[32,1,6]{2,1,0:T(1,128)}), s32[32,1,6]{2,1,0:T(1,128)S(1)}, u32[]{:S(2)}, u32[]{:S(2)}) %all-to-all-start) | async-done | bytes 800 | tf_op jit(solution)/shard_map/all_to_all | solution.py:41
  31.6 0.1 reshape.180
  31.8 0.7 gather_fusion
  32.5 0.1 reshape.179
  32.7 0.6 copy.32
  33.3 3.9 all-to-all-start.1
  37.2 7.9 %gather_fusion.2 = bf16[192,2,128,128]{3,2,1,0:T(8,128)(2,1)} fusion(bf16[48,2,128,128]{3,2,1,0:T(8,128)(2,1)S(1)} %copy-done, s32[1024]{0:T(1024)S(1)} %pad_clamp_fusion.1), kind=kCustom, calls=%fused_computation.2 | custom fusion | bytes 25166592 | tf_op jit(solution)/shard_map/gather | solution.py:43
  45.1 0.7 all-to-all-done.1
  45.8 8.9 %all-to-all-start.2 = ((bf16[32,6,2,128,128]{4,3,2,1,0:T(8,128)(2,1)}), bf16[32,6,2,128,128]{4,3,2,1,0:T(8,128)(2,1)}, u32[]{:S(2)}, u32[]{:S(2)}) async-start(bf16[32,6,2,128,128]{4,3,2,1,0:T(8,128)(2,1)} %bitcast.66), calls=%async_computation.2 | async-start | bytes 25165824 | tf_op jit(solution)/shard_map/all_to_all | solution.py:43
  54.7 0.3 reduce-scatter.2.cloned.1.call-start
  55.1 0.1 reshape.173
  55.2 0.1 copy.34
  55.4 0.6 gather_fusion.1
  56.0 0.1 broadcast_add_fusion
  56.1 0.2 add.122
  56.3 280.3 %all-to-all-done.2 = bf16[32,6,2,128,128]{4,3,2,1,0:T(8,128)(2,1)} async-done(((bf16[32,6,2,128,128]{4,3,2,1,0:T(8,128)(2,1)}), bf16[32,6,2,128,128]{4,3,2,1,0:T(8,128)(2,1)}, u32[]{:S(2)}, u32[]{:S(2)}) %all-to-all-start.2) | async-done | bytes 12582944 | tf_op jit(solution)/shard_map/all_to_all | solution.py:43
  336.6 10.5 %gather_fusion.3 = bf16[96,2,128,128]{3,2,1,0:T(8,128)(2,1)} fusion(bf16[192,2,128,128]{3,2,1,0:T(8,128)(2,1)} %bitcast.6, s32[1024]{0:T(1024)S(1)} %pad_clamp_fusion), kind=kCustom, calls=%fused_computation.3 | custom fusion | bytes 12583296 | tf_op jit(solution)/shard_map/gather | solution.py:46
  347.1 8.3 %convolution_convert_fusion = bf16[96,2,128,128]{3,2,1,0:T(8,128)(2,1)} fusion(bf16[96,2,128,128]{3,2,1,0:T(8,128)(2,1)} %gather_fusion.3, bf16[96,128,128,1]{2,1,3,0:T(8,128)(2,1)} %bitcast.69), kind=kOutput, calls=%fused_computation.8 | convolution fusion | flops 808452096 | bytes 15728640 | tf_op jit(solution)/shard_map/nab,ntbc->ntac/dot_general | solution.py:48
  355.4 14.5 %convolution_bitcast_fusion = f32[48,2,2,2,128,128]{4,5,2,3,1,0:T(8,128)} fusion(bf16[48,2,2,128,128,1]{3,4,5,2,1,0:T(8,128)(2,1)} %bitcast.67, bf16[48,2,128,128]{3,2,1,0:T(8,128)(2,1)S(1)} %copy-done), kind=kOutput, calls=%fused_computation.7 | convolution fusion | flops 1610612736 | bytes 34603008 | tf_op jit(solution)/shard_map/rsba,rktbc->rkstac/dot_general | solution.py:52
  369.9 24.7 %copy.36 = f32[48,2,2,2,128,128]{5,4,3,2,1,0:T(8,128)} copy(f32[48,2,2,2,128,128]{4,5,2,3,1,0:T(8,128)} %convolution_bitcast_fusion) | data formatting | bytes 50331648 | tf_op jit(solution)/shard_map/rsba,rktbc->rkstac/transpose | solution.py:52
  394.6 25.7 %copy.46 = f32[48,8,128,128]{3,1,2,0:T(8,128)} copy(f32[48,8,128,128]{3,2,1,0:T(8,128)} %bitcast.65) | data formatting | bytes 50331648
  420.3 58.0 %scatter_custom_fusion.1 = f32[96,16384]{1,0:T(8,128)} fusion(s32[384]{0:T(512)S(1)} %fusion.5, f32[384,16384]{1,0:T(8,128)} %bitcast.68, f32[]{:T(128)} %constant.29.clone.1), kind=kCustom, calls=%fused_computation.10 | custom fusion | flops 6291456 | bytes 6291968 | tf_op jit(solution)/shard_map/scatter-add | solution.py:59
  478.3 3.3 slice_bitcast_fusion.1
  481.5 0.4 copy.43
  481.9 0.4 copy.44
  482.3 11.3 %collective-permute-start.1 = (f32[1,32,128,128]{3,2,1,0:T(8,128)S(1)}, f32[1,32,128,128]{3,2,1,0:T(8,128)S(1)}, u32[]{:S(2)}, u32[]{:S(2)}) collective-permute-start(f32[1,32,128,128]{3,2,1,0:T(8,128)S(1)} %bitcast.71), channel_id=1, source_target_pairs={{8,0},{16,8},{24,16},{32,24},{40,32},{48,40},{56,48},{64,56},{72,6... | collective-permute-start | bytes 6291464 | tf_op jit(solution)/shard_map/ppermute | solution.py:16
  493.6 0.4 copy.42
  494.0 42.8 %collective-permute-done.1 = f32[1,32,128,128]{3,2,1,0:T(8,128)S(1)} collective-permute-done((f32[1,32,128,128]{3,2,1,0:T(8,128)S(1)}, f32[1,32,128,128]{3,2,1,0:T(8,128)S(1)}, u32[]{:S(2)}, u32[]{:S(2)}) %collective-permute-start.1) | collective-permute-done | bytes 2097184 | tf_op jit(solution)/shard_map/ppermute | solution.py:16
  536.8 5.2 collective-permute-done
  542.0 1.9 fusion.3
  543.9 35.6 %reduce-scatter.2.cloned.1.call-done = f32[4,128,128]{2,1,0:T(8,128)} async-done(((f32[32,128,128]{2,1,0:T(8,128)}), f32[4,128,128]{2,1,0:T(8,128)}) %reduce-scatter.2.cloned.1.call-update) | async-done | bytes 262160 | tf_op jit(solution)/shard_map/reduce_scatter | solution.py:62
  579.6 1.6 convert_bitcast_fusion
  (20 shorter events, 0.4 us)
Async XLA Ops:
  6.5 30.6 %copy-start = (bf16[48,2,128,128]{3,2,1,0:T(8,128)(2,1)S(1)}, bf16[48,2,128,128]{3,2,1,0:T(8,128)(2,1)}, u32[]{:S(2)}) copy-start(bf16[48,2,128,128]{3,2,1,0:T(8,128)(2,1)} %param.6) | copy-start | bytes 9437188
  11.3 20.4 %all-to-all-start = ((s32[32,1,6]{2,1,0:T(1,128)}), s32[32,1,6]{2,1,0:T(1,128)S(1)}, u32[]{:S(2)}, u32[]{:S(2)}) async-start(s32[32,1,6]{2,1,0:T(1,128)} %bitcast.2), calls=%async_computation | async-start | bytes 32768 | tf_op jit(solution)/shard_map/all_to_all | solution.py:41
  33.3 12.5 %all-to-all-start.1 = ((s32[32,6,2]{1,2,0:T(2,128)}), s32[32,6,2]{1,2,0:T(2,128)S(1)}, u32[]{:S(2)}, u32[]{:S(2)}) async-start(s32[32,6,2]{1,2,0:T(2,128)} %copy.32), calls=%async_computation.1 | async-start | bytes 65536 | tf_op jit(solution)/shard_map/all_to_all | solution.py:44
  45.8 9.2 %copy-start.2 = (s32[48,2]{0,1:T(2,128)S(1)}, s32[48,2]{0,1:T(2,128)}, u32[]{:S(2)}) copy-start(s32[48,2]{0,1:T(2,128)} %param.7) | copy-start | bytes 1156
  45.8 290.8 %all-to-all-start.2 = ((bf16[32,6,2,128,128]{4,3,2,1,0:T(8,128)(2,1)}), bf16[32,6,2,128,128]{4,3,2,1,0:T(8,128)(2,1)}, u32[]{:S(2)}, u32[]{:S(2)}) async-start(bf16[32,6,2,128,128]{4,3,2,1,0:T(8,128)(2,1)} %bitcast.66), calls=%async_computation.2 | async-start | bytes 25165824 | tf_op jit(solution)/shard_map/all_to_all | solution.py:43
  54.7 524.9 %reduce-scatter.2.cloned.1.call-start = ((), (), s32[]{:S(2)}) async-start(), calls=%async_computation.4 | async-start | bytes 2359296 | tf_op jit(solution)/shard_map/reduce_scatter | solution.py:62
  482.3 54.5 %collective-permute-start.1 = (f32[1,32,128,128]{3,2,1,0:T(8,128)S(1)}, f32[1,32,128,128]{3,2,1,0:T(8,128)S(1)}, u32[]{:S(2)}, u32[]{:S(2)}) collective-permute-start(f32[1,32,128,128]{3,2,1,0:T(8,128)S(1)} %bitcast.71), channel_id=1, source_target_pairs={{8,0},{16,8},{24,16},{32,24},{40,32},{48,40},{56,48},{64,56},{72,6... | collective-permute-start | bytes 6291464 | tf_op jit(solution)/shard_map/ppermute | solution.py:16
  493.6 48.4 %collective-permute-start = (f32[1,32,128,128]{3,2,1,0:T(8,128)S(1)}, f32[1,32,128,128]{3,2,1,0:T(8,128)S(1)}, u32[]{:S(2)}, u32[]{:S(2)}) collective-permute-start(f32[1,32,128,128]{3,2,1,0:T(8,128)S(1)} %bitcast.70), channel_id=1, source_target_pairs={{0,8},{8,16},{16,24},{24,32},{32,40},{40,48},{48,56},{56,64},{64,7... | collective-permute-start | bytes 6291464 | tf_op jit(solution)/shard_map/ppermute | solution.py:14
  493.6 87.6 %copy-start.1 = (bf16[48,2,128,128]{3,2,1,0:T(8,128)(2,1)S(1)}, bf16[48,2,128,128]{3,2,1,0:T(8,128)(2,1)}, u32[]{:S(2)}) copy-start(bf16[48,2,128,128]{3,2,1,0:T(8,128)(2,1)} %param.6) | copy-start | bytes 9437188
Sparse Core Ops, SparseCore 0:
  544.0 35.4 reduce-scatter.1
where the time goes:
time: 595 us; the launch traced here: 588 us
  waiting for transfers between devices  372 us (63%)
  local copies, waits for them, and re-layouts  79.4 us (13%)
  other arithmetic  63.7 us (11%)
  starting transfers between devices  36.2 us (6%)
  matrix products  22.8 us (4%)
  between operations  14 us (2%)
    all_to_all x1, waiting for transfers between devices, local(): lax.all_to_all(p_tiles[wanted], 'grid', split_axis=0, concat_axis=0, tile...  280 us
    scatter-add x1, other arithmetic, local(): partials.at[targets]  58 us
    ppermute x1, waiting for transfers between devices, with_halo(): lax.ppermute(head, axis, [((i + 1) % count, i) for i in range(count)])  42.8 us
    reduce_scatter x1, waiting for transfers between devices, local(): lax.psum_scatter(with_rims[2] + with_rims[0] + with_rims[4], 'layer', sca...  35.6 us
    unnamed x12, local copies, waits for them, and re-layouts  30.9 us
    transpose x1, local copies, waits for them, and re-layouts, local(): jnp.einsum('rsba,rktbc->rkstac', p_tiles, products, preferred_element_typ...  24.7 us
    dot_general x1, matrix products, local(): jnp.einsum('rsba,rktbc->rkstac', p_tiles, products, preferred_element_typ...  14.5 us
  transfers between devices with their start and end apart: 6, of which 6 were waited for; matrix products, arithmetic and copies ran while one was open for 2% of the time, Pallas kernels for 0%

commit v1 on v0

v1 whole, which is shorter than its diff:
```python
import functools

import jax
import jax.numpy as jnp
from jax import lax
from jax.experimental import pallas as pl
from jax.experimental.pallas import tpu as pltpu
from jax.sharding import PartitionSpec as P

MESH = pl.DeviceIdType.MESH
SHIFT = 64
CHUNK = 4
LAG = 2


def bucket_kernel(cap, fine_rows, per_layer, a_cols, perm, meta):
    layers, owner_slots = meta.shape[0], perm.shape[0]
    owners = owner_slots // cap
    per = owners // layers * cap

    def clear(s, unused):
        perm[s] = 0
        meta[s // per, 0, s % per] = fine_rows * SHIFT
        return unused

    lax.fori_loop(0, owner_slots, clear, 0)

    def scoped(count):
        def zero(g, unused):
            count[g] = 0
            return unused

        lax.fori_loop(0, owners, zero, 0)

        def place(r, unused):
            for k in range(per_layer):
                col = a_cols[r, k]
                owner = col // fine_rows
                at = owner * cap + count[owner]
                count[owner] = count[owner] + 1
                perm[at] = r * per_layer + k
                meta[at // per, 0, at % per] = r * SHIFT + (col - owner * fine_rows)
            return unused

        lax.fori_loop(0, fine_rows, place, 0)

    pl.run_scoped(scoped, pltpu.SMEM((owners,), jnp.int32))


def main_kernel(
    nz, nx, nl, cap,
    perm, pc_s, a_hbm, p_hbm, meta_v, pc_v, out_ref,
    a_vm, p_own, asend, arecv, metar, meta_s, pbuf, pcbuf, pcs, ptw, wide, tot, hsend_i, hsend_c, hrecv_i, hrecv_c,
    load_sem, as_sem, ar_sem, ms_sem, mr_sem, zs, zr, xs, xr, fs, fr, pcss, pcr, hs, hr,
):
    fine = p_own.shape[0]
    half = fine // 2
    chunks = half // CHUNK
    nq = nx
    layer = lax.axis_index("layer")
    grid = lax.axis_index("grid")
    z, x = grid // nx, grid % nx
    d = lax.rem(z - layer + nz, nz)
    up = lax.rem(z + 1, nz) * nx + x
    down = lax.rem(z + nz - 1, nz) * nx + x
    right = z * nx + lax.rem(x + 1, nx)
    left = z * nx + lax.rem(x + nx - 1, nx)
    after, before = lax.rem(grid + 1, nz * nx), lax.rem(grid + nz * nx - 1, nz * nx)
    lafter, lbefore = lax.rem(layer + 1, nl), lax.rem(layer + nl - 1, nl)

    def remote(src, dst, ssem, rsem, g, l):
        return pltpu.make_async_remote_copy(
            src_ref=src, dst_ref=dst, send_sem=ssem, recv_sem=rsem, device_id=(g, l), device_id_type=MESH
        )

    load_a = pltpu.make_async_copy(a_hbm, a_vm, load_sem.at[0])
    load_p = pltpu.make_async_copy(p_hbm, p_own, load_sem.at[1])
    load_p.start()
    load_a.start()

    @pl.when(d == 0)
    def _():
        first = pltpu.make_async_copy(p_hbm, pbuf.at[0], load_sem.at[2])
        first.start()
        first.wait()
        cols = pltpu.make_async_copy(pc_v, pcbuf.at[0], load_sem.at[2])
        cols.start()
        cols.wait()

    barrier = pltpu.get_barrier_semaphore()
    partners = [(up, layer), (down, layer), (right, layer), (left, layer)]
    partners += [(grid, lax.rem(layer + k, nl)) for k in range(1, nl)]
    partners += [(g, l) for g in (after, before) for l in (layer, lafter, lbefore)]
    for g, l in partners:
        pl.semaphore_signal(barrier, inc=1, device_id=(g, l), device_id_type=MESH)
    pl.semaphore_wait(barrier, len(partners))

    load_a.wait()

    per = nq * cap

    def bucket(to):
        def one(s, unused):
            g = to * nq + s // cap
            asend[g, s % cap] = a_vm[perm[to * per + s]]
            return unused

        lax.fori_loop(0, per, one, 0)

    def a_copy(k):
        to = lax.rem(layer + k, nl)
        return remote(asend.at[pl.ds(to * nq, nq)], arecv.at[layer], as_sem.at[k], ar_sem.at[k], grid, to)

    def m_copy(k):
        to = lax.rem(layer + k, nl)
        return remote(meta_v.at[to], metar.at[layer], ms_sem.at[k], mr_sem.at[k], grid, to)

    def send_a(k, unused):
        to = lax.rem(layer + k, nl)
        bucket(to)
        a_copy(k).start()
        m_copy(k).start()
        return unused

    lax.fori_loop(1, nl, send_a, 0)
    bucket(layer)
    own_a = pltpu.make_async_copy(asend.at[pl.ds(layer * nq, nq)], arecv.at[layer], load_sem.at[2])
    own_a.start()
    own_m = pltpu.make_async_copy(meta_v.at[layer], metar.at[layer], load_sem.at[3])
    own_m.start()
    load_p.wait()

    def block(rel, s, c):
        return pbuf.at[rel, pl.ds(s * half + c * CHUNK, CHUNK)]

    def z_copy(s, c):
        blk = block(0, s, c)
        return remote(blk, blk, zs.at[s, c], zr.at[s, c], (up, down)[s], layer)

    def x_copy(side, s, c):
        return remote(
            block(0, s, c), block((3, 1)[side], s, c), xs.at[side, s, c], xr.at[side, s, c], (right, left)[side], layer
        )

    def f_copy(s, c):
        return remote(block((3, 1)[s], s, c), block(2, s, c), fs.at[s, c], fr.at[s, c], (right, left)[s], layer)

    def pc_copy(which):
        src, dst, g = ((0, 0, up), (0, 3, right), (0, 1, left), (3, 2, right))[which]
        return remote(pcbuf.at[src], pcbuf.at[dst], pcss.at[which], pcr.at[which], g, layer)

    def transpose_rows(lo):
        for r in range(4):
            i = lo * 4 + r
            o0 = lax.rem(pc_s[i, 0] - grid + 1 + nz * nx, nz * nx)
            o1 = lax.rem(pc_s[i, 1] - grid + 1 + nz * nx, nz * nx)
            t0 = p_own[i, 0].T
            t1 = p_own[i, 1].T
            zero = jnp.zeros_like(t0)
            for b in range(3):
                ptw[i, b * 128 : (b + 1) * 128, :] = jnp.where(o0 == b, t0, jnp.where(o1 == b, t1, zero))

    ptw[fine] = jnp.zeros(ptw.shape[1:], ptw.dtype)

    steps = chunks + nz + LAG

    def step(t, unused):
        for s in (0, 1):
            hop = d if s == 0 else lax.rem(nz - d, nz)
            c = t - hop

            @pl.when((c >= 0) & (c < chunks))
            def _():
                @pl.when(d != 0)
                def _():
                    z_copy(s, c).wait_recv()

                @pl.when(hop < nz - 1)
                def _():
                    z_copy(s, c).start()

                x_copy(0, s, c).start()
                x_copy(1, s, c).start()
                if s == 0:

                    @pl.when(c == 0)
                    def _():
                        @pl.when(d != 0)
                        def _():
                            pc_copy(0).wait_recv()

                        @pl.when(hop < nz - 1)
                        def _():
                            pc_copy(0).start()

                        pc_copy(1).start()
                        pc_copy(2).start()

            f = c - LAG

            @pl.when((f >= 0) & (f < chunks))
            def _():
                x_copy(s, s, f).wait_recv()
                f_copy(s, f).start()
                if s == 0:

                    @pl.when(f == 0)
                    def _():
                        pc_copy(1).wait_recv()
                        pc_copy(3).start()

        @pl.when(t < fine // 4)
        def _():
            transpose_rows(t)

        return unused

    lax.fori_loop(0, max(steps, fine // 4), step, 0)

    def a_wait(k, unused):
        a_copy(k).wait_recv()
        m_copy(k).wait_recv()
        return unused

    lax.fori_loop(1, nl, a_wait, 0)
    own_a.wait()
    own_m.wait()
    pc_copy(2).wait_recv()
    pc_copy(3).wait_recv()
    tables = pltpu.make_async_copy(metar, meta_s, load_sem.at[2])
    tables.start()
    tables.wait()
    tables = pltpu.make_async_copy(pcbuf, pcs, load_sem.at[2])
    tables.start()
    tables.wait()

    tot[...] = jnp.zeros_like(tot)
    slots = nl * cap
    group = 4

    def accumulate(rel):
        q = lax.rem(x + rel, nx)
        owner = layer * nq + q

        def widen(j, unused):
            o0 = lax.rem(pcs[rel, 0, 2 * j] - owner + 1 + nz * nx, nz * nx)
            o1 = lax.rem(pcs[rel, 0, 2 * j + 1] - owner + 1 + nz * nx, nz * nx)
            t0 = pbuf[rel, j, 0]
            t1 = pbuf[rel, j, 1]
            zero = jnp.zeros_like(t0)
            for b in range(3):
                wide[j, :, b * 128 : (b + 1) * 128] = jnp.where(o0 == b, t0, jnp.where(o1 == b, t1, zero))
            return unused

        lax.fori_loop(0, fine, widen, 0)

        def some(u, acc):
            lefts, prods = [], []
            for v in range(group):
                n = u * group + v
                src, k = n // cap, n % cap
                m = meta_s[src, 0, q * cap + k]
                i, j = m // SHIFT, m % SHIFT
                prods.append(
                    jnp.dot(arecv[src, q, k], wide[j], preferred_element_type=jnp.float32).astype(jnp.bfloat16)
                )
                lefts.append(ptw[i])
            return acc + jnp.dot(
                jnp.concatenate(lefts, axis=1), jnp.concatenate(prods, axis=0), preferred_element_type=jnp.float32
            )

        acc = lax.fori_loop(0, slots // group, some, jnp.zeros((384, 384), jnp.float32))
        for a in range(3):
            for b in range(3):
                tot[a, q + b] += acc[a * 128 : (a + 1) * 128, b * 128 : (b + 1) * 128]

    accumulate(0)

    def wait_rest(side):
        def one(c, unused):
            x_copy(side, 1 - side, c).wait_recv()
            return unused

        lax.fori_loop(0, chunks, one, 0)

    wait_rest(0)
    accumulate(3)
    wait_rest(1)
    accumulate(1)

    def wait_forward(c, unused):
        f_copy(0, c).wait_recv()
        f_copy(1, c).wait_recv()
        return unused

    lax.fori_loop(0, chunks, wait_forward, 0)
    accumulate(2)

    bf = jnp.bfloat16
    hsend_i[0] = tot[2, 1 : nq + 1].astype(bf)
    hsend_i[1] = tot[0, 1 : nq + 1].astype(bf)
    hsend_c[0] = tot[1, nq + 1].astype(bf)
    hsend_c[1] = tot[1, 0].astype(bf)
    hsend_c[2] = tot[2, nq + 1].astype(bf)
    hsend_c[3] = tot[2, 0].astype(bf)
    hsend_c[4] = tot[0, nq + 1].astype(bf)
    hsend_c[5] = tot[0, 0].astype(bf)
    copies = [
        remote(hsend_i.at[k], hrecv_i.at[k], hs.at[k], hr.at[k], g, layer) for k, g in enumerate((after, before))
    ]
    to = [(g, l) for g in (grid, after, before) for l in (lafter, lbefore)]
    copies += [
        remote(hsend_c.at[k], hrecv_c.at[k], hs.at[2 + k], hr.at[2 + k], g, l) for k, (g, l) in enumerate(to)
    ]
    for copy in copies:
        copy.start()
    for copy in copies:
        copy.wait_recv()
    for b in range(nq):
        total = tot[1, 1 + b]
        for k in range(2):
            total = total + hrecv_i[k, b].astype(jnp.float32)
        if b == 0:
            for k in (0, 2, 4):
                total = total + hrecv_c[k].astype(jnp.float32)
        if b == nq - 1:
            for k in (1, 3, 5):
                total = total + hrecv_c[k].astype(jnp.float32)
        out_ref[0, b] = total.astype(bf)

    for copy in copies:
        copy.wait_send()

    def a_sent(k, unused):
        a_copy(k).wait_send()
        m_copy(k).wait_send()
        return unused

    lax.fori_loop(1, nl, a_sent, 0)

    def sent(c, unused):
        for s in (0, 1):
            hop = d if s == 0 else lax.rem(nz - d, nz)

            @pl.when(hop < nz - 1)
            def _():
                z_copy(s, c).wait_send()

            x_copy(0, s, c).wait_send()
            x_copy(1, s, c).wait_send()
            f_copy(s, c).wait_send()
        return unused

    lax.fori_loop(0, chunks, sent, 0)

    @pl.when(d < nz - 1)
    def _():
        pc_copy(0).wait_send()

    for which in (1, 2, 3):
        pc_copy(which).wait_send()


def local(nx, a_tiles, a_cols, p_tiles, p_cols):
    fine, per_layer, size, unused = a_tiles.shape
    nl, ng = lax.axis_size("layer"), lax.axis_size("grid")
    nz = ng // nx
    cap = 2 * fine * per_layer // ng
    smem = pl.BlockSpec(memory_space=pltpu.SMEM)
    anywhere = pl.BlockSpec(memory_space=pl.ANY)
    perm, meta = pl.pallas_call(
        functools.partial(bucket_kernel, cap, fine, per_layer),
        out_shape=(
            jax.ShapeDtypeStruct((ng * cap,), jnp.int32),
            jax.ShapeDtypeStruct((nl, 1, 128), jnp.int32),
        ),
        in_specs=[smem],
        out_specs=(smem, smem),
    )(a_cols)
    pc_flat = jnp.pad(p_cols.reshape(1, -1), ((0, 0), (0, 128 - 2 * fine)))
    chunks = fine // 2 // CHUNK
    bf, f32, i32 = jnp.bfloat16, jnp.float32, jnp.int32
    dma = pltpu.SemaphoreType.DMA
    return pl.pallas_call(
        functools.partial(main_kernel, nz, nx, nl, cap),
        out_shape=jax.ShapeDtypeStruct((1, nx, size, size), bf),
        in_specs=[smem, smem, anywhere, anywhere, anywhere, anywhere],
        out_specs=pl.BlockSpec(memory_space=pltpu.VMEM),
        scratch_shapes=[
            pltpu.VMEM((fine * per_layer, size, size), bf),
            pltpu.VMEM(p_tiles.shape, bf),
            pltpu.VMEM((ng, cap, size, size), bf),
            pltpu.VMEM((nl, nx, cap, size, size), bf),
            pltpu.VMEM((nl, 1, 128), i32),
            pltpu.SMEM((nl, 1, 128), i32),
            pltpu.VMEM((nx,) + p_tiles.shape, bf),
            pltpu.VMEM((nx, 1, 128), i32),
            pltpu.SMEM((nx, 1, 128), i32),
            pltpu.VMEM((fine + 1, 3 * size, size), bf),
            pltpu.VMEM((fine, size, 3 * size), bf),
            pltpu.VMEM((3, nx + 2, size, size), f32),
            pltpu.VMEM((2, nx, size, size), bf),
            pltpu.VMEM((6, size, size), bf),
            pltpu.VMEM((2, nx, size, size), bf),
            pltpu.VMEM((6, size, size), bf),
            dma((4,)),
            dma((nl,)), dma((nl,)), dma((nl,)), dma((nl,)),
            dma((2, chunks)), dma((2, chunks)),
            dma((2, 2, chunks)), dma((2, 2, chunks)),
            dma((2, chunks)), dma((2, chunks)),
            dma((4,)), dma((4,)),
            dma((8,)), dma((8,)),
        ],
        compiler_params=pltpu.CompilerParams(
            collective_id=0, has_side_effects=True, vmem_limit_bytes=56 * 1024 * 1024
        ),
    )(perm, p_cols, a_tiles.reshape(fine * per_layer, size, size), p_tiles, meta, pc_flat)


def solution(mesh):
    nx = 4
    return jax.shard_map(
        functools.partial(local, nx),
        mesh=mesh,
        in_specs=(
            P("grid", "layer", None, None),
            P("grid", "layer"),
            P("grid", None, None, None),
            P("grid", None),
        ),
        out_specs=P("grid", "layer", None, None),
        check_vma=False,
    )
```

time: 595 us -> 189 us (0.32)
  the two profiles are of different devices: /device:TPU:1 before, /device:TPU:41 now
where the time goes in v1:
time: 189 us
  Pallas kernels  185 us (98%)
  local copies, waits for them, and re-layouts  4.35 us (2%)
    pallas_call x1, Pallas kernels, local(): pl.pallas_call(functools.partial(main_kernel, nz, nx, nl, cap), out_shape...  178 us
    pallas_call x1, Pallas kernels, local(): pl.pallas_call(functools.partial(bucket_kernel, cap, fine, per_layer), ou...  6.94 us

profile of v1, /device:TPU:41, one launch (start us, length us, event | category | flops | bytes accessed | tf_op | source)
XLA Modules:
  0.0 189.0 jit_solution(2714392208277093842)
XLA Ops:
  0.0 0.8 copy.10.pc_s
  0.8 0.0 copy-start
  0.8 0.1 reshape.7
  0.9 0.5 pad.4.pc_v
  1.4 1.4 copy.8.a_cols
  2.8 6.9 %shard_map.46 = (s32[192]{0:T(256)}, s32[8,1,128]{2,1,0:T(1,128)}) custom-call(s32[48,2]{1,0:T(8,128)} %copy.8.a_cols), custom_call_target="tpu_custom_call" | custom-call | tf_op jit(solution)/shard_map/pallas_call | solution.py:371
  9.7 0.0 copy-done
  9.7 177.6 %shard_map.47 = bf16[1,4,128,128]{3,2,1,0:T(8,128)(2,1)} custom-call(s32[192]{0:T(256)} %get-tuple-element.7.perm, s32[48,2]{1,0:T(8,128)} %copy-done, bf16[96,128,128]{2,1,0:T(8,128)(2,1)} %bitcast.1, bf16[48,2,128,128]{3,2,1,0:T(8,128)(2,1)} %p_hbm.1, s32[8,1,128]{2,1,0:T(1,128)} %get-tuple-element.8.meta_v, s32[1,128]{1,0:T(1,128)} %pad.4.pc_v), custom_call_target="tpu_custom_call" | custom-call | tf_op jit(solution)/shard_map/pallas_call | solution.py:384
  187.4 1.6 copy.12
Async XLA Ops:
  0.8 9.0 %copy-start = (s32[48,2]{1,0:T(8,128)}, s32[48,2]{1,0:T(8,128)S(1)}, u32[]{:S(2)}) copy-start(s32[48,2]{1,0:T(8,128)S(1)} %copy.10.pc_s) | copy-start | bytes 1156

commit v2 on v1

v2 whole, which is shorter than its diff:
```python
import functools

import jax
import jax.numpy as jnp
from jax import lax
from jax.experimental import pallas as pl
from jax.experimental.pallas import tpu as pltpu
from jax.sharding import PartitionSpec as P

MESH = pl.DeviceIdType.MESH
SHIFT = 64
CHUNK = 1
LAG = 3
PASS = 0
PLANE_ROWS = 16
HOP = 3
GROUP = 8
WIDEN = 12


def main_kernel(
    nz, nx, nl, cap, per_layer,
    tab, a_hbm, p_hbm, out_ref,
    tabv, tabs, permv, perms, a_vm, p_own, asend, arecv, metav, metar, meta_s, pbuf, pcbuf, pcs, ptw, wide, acc, tot,
    hsend_i, hsend_c, hrecv_i, hrecv_c,
    load_sem, as_sem, ar_sem, ms_sem, mr_sem, zs, zr, xs, xr, fs, fr, rs, rr, gs, gr, pcss, pcr, hs, hr,
):
    fine = p_own.shape[0]
    half = fine // 2
    late = PLANE_ROWS // 2
    early = half - late
    early_chunks, late_chunks = early // CHUNK, late // CHUNK
    chunks = early_chunks + nx * late_chunks
    ng = nz * nx
    layer = lax.axis_index("layer")
    grid = lax.axis_index("grid")
    z, x = grid // nx, grid % nx
    d = lax.rem(z - layer + nz, nz)
    up = lax.rem(z + 1, nz) * nx + x
    down = lax.rem(z + nz - 1, nz) * nx + x
    right = z * nx + lax.rem(x + 1, nx)
    left = z * nx + lax.rem(x + nx - 1, nx)
    after, before = lax.rem(grid + 1, ng), lax.rem(grid + ng - 1, ng)
    lafter, lbefore = lax.rem(layer + 1, nl), lax.rem(layer + nl - 1, nl)

    def remote(src, dst, ssem, rsem, g, l):
        return pltpu.make_async_remote_copy(
            src_ref=src, dst_ref=dst, send_sem=ssem, recv_sem=rsem, device_id=(g, l), device_id_type=MESH
        )

    def turn(o):
        return o + o // 2 * (1 - 2 * (o % 2))

    load_p = pltpu.make_async_copy(p_hbm, p_own, load_sem.at[1])
    load_a = pltpu.make_async_copy(a_hbm, a_vm, load_sem.at[0])
    load_t = pltpu.make_async_copy(tab, tabv, load_sem.at[2])
    load_s = pltpu.make_async_copy(tab, tabs, load_sem.at[3])
    first = pltpu.make_async_copy(p_hbm, pbuf.at[0], load_sem.at[4])
    cols = pltpu.make_async_copy(tab.at[2], pcbuf.at[0], load_sem.at[5])

    @pl.when(d == 0)
    def _():
        first.start()
        cols.start()

    load_t.start()
    load_s.start()
    load_a.start()
    load_p.start()

    barrier = pltpu.get_barrier_semaphore()
    partners = [(up, layer), (down, layer), (right, layer), (left, layer)]
    partners += [(grid, lax.rem(layer + k, nl)) for k in range(1, nl)]
    partners += [(g, l) for g in (after, before) for l in (layer, lafter, lbefore)]
    for g, l in partners:
        pl.semaphore_signal(barrier, inc=1, device_id=(g, l), device_id_type=MESH)
    pl.semaphore_wait(barrier, len(partners))

    @pl.when(d == 0)
    def _():
        first.wait()
        cols.wait()

    def early_block(rel, s, c):
        return pbuf.at[rel, pl.ds(s * half + c * CHUNK, CHUNK)]

    def late_block(rel, s):
        return pbuf.at[rel, pl.ds(s * half + early, late)]

    def z_copy(s, c):
        e = jnp.maximum(c - early_chunks, 0)
        is_late = jnp.minimum(jnp.maximum(c - early_chunks + 1, 0), 1)
        rel = turn(e // late_chunks)
        row = s * half + is_late * (early + e % late_chunks * CHUNK) + (1 - is_late) * c * CHUNK
        blk = pbuf.at[rel, pl.ds(row, CHUNK)]
        return remote(blk, blk, zs.at[s, c], zr.at[s, c], (up, down)[s], layer)

    def x_copy(side, s, c):
        return remote(
            early_block(0, s, c), early_block((3, 1)[side], s, c), xs.at[side, s, c], xr.at[side, s, c],
            (right, left)[side], layer,
        )

    def f_copy(s, c):
        return remote(
            early_block((3, 1)[s], s, c), early_block(2, s, c), fs.at[s, c], fr.at[s, c], (right, left)[s], layer
        )

    def r_copy(side, s):
        return remote(
            late_block(0, s), late_block((3, 1)[side], s), rs.at[side, s], rr.at[side, s], (right, left)[side], layer
        )

    def g_copy(s):
        return remote(late_block((3, 1)[s], s), late_block(2, s), gs.at[s], gr.at[s], (right, left)[s], layer)

    def pc_copy(which):
        src, dst, g = ((0, 0, up), (0, 3, right), (0, 1, left), (3, 2, right))[which]
        return remote(pcbuf.at[src], pcbuf.at[dst], pcss.at[which], pcr.at[which], g, layer)

    hops = (d, lax.rem(nz - d, nz))
    near, far = jnp.minimum(*hops), jnp.maximum(*hops)
    near_turn = HOP * near
    far_turn = jnp.maximum(near_turn + early_chunks, HOP * far)
    up_first = jnp.minimum(jnp.maximum(hops[1] - hops[0] + 1, 0), 1)
    x_turn = (
        up_first * near_turn + (1 - up_first) * far_turn,
        up_first * far_turn + (1 - up_first) * near_turn,
    )
    pass_turn = jnp.maximum(far_turn + early_chunks + LAG, chunks + PASS)
    ready = jnp.maximum(early_chunks + late_chunks + HOP * far, pass_turn + early_chunks - late_chunks)

    def p_step(t):
        for s in (0, 1):
            hop = hops[s]
            c = t - HOP * hop

            @pl.when((c >= 0) & (c < chunks))
            def _():
                @pl.when(d != 0)
                def _():
                    z_copy(s, c).wait_recv()

                @pl.when(d == 0)
                def _():
                    @pl.when(c == early_chunks + (1 + s) * late_chunks)
                    def _():
                        r_copy(1 - s, s).wait_recv()

                    @pl.when(c == early_chunks + 3 * late_chunks)
                    def _():
                        g_copy(s).wait_recv()

                @pl.when(hop < nz - 1)
                def _():
                    z_copy(s, c).start()

                if s == 0:

                    @pl.when(c == 0)
                    def _():
                        @pl.when(d != 0)
                        def _():
                            pc_copy(0).wait_recv()

                        @pl.when(hop < nz - 1)
                        def _():
                            pc_copy(0).start()

                        pc_copy(1).start()
                        pc_copy(2).start()

                    @pl.when(c == 2)
                    def _():
                        pc_copy(1).wait_recv()
                        pc_copy(3).start()

                @pl.when((d == 0) & (c == 0))
                def _():
                    r_copy(0, s).start()
                    r_copy(1, s).start()

                @pl.when((d == 0) & (c == early_chunks))
                def _():
                    r_copy(s, s).wait_recv()
                    g_copy(s).start()

            e = t - x_turn[s]

            @pl.when((e >= 0) & (e < early_chunks))
            def _():
                x_copy(0, s, e).start()
                x_copy(1, s, e).start()

        f = t - pass_turn

        @pl.when((f >= 0) & (f < early_chunks))
        def _():
            for s in (0, 1):
                x_copy(s, s, f).wait_recv()
                f_copy(s, f).start()

    p_step(0)

    load_t.wait()
    size = tabv.shape[2]
    per = nx * cap
    blank = fine * SHIFT
    rows = lax.broadcasted_iota(jnp.int32, (size, size), 0)
    lanes = lax.broadcasted_iota(jnp.int32, (size, size), 1)

    def upright(v):
        return jnp.broadcast_to(v, (size, size)).T

    own = tabv[0]
    same = (upright(own) == jnp.broadcast_to(own, (size, size))) & (rows < lanes)
    rank = jnp.sum(jnp.where(same, 1, 0), axis=0, keepdims=True)
    slot = upright(own * cap + rank)
    value = upright(tabv[1] - blank)
    for l in range(nl):
        hit = (slot == l * per + lanes) & (lanes < per) & (rows < a_vm.shape[0])
        permv[l] = jnp.sum(jnp.where(hit, rows, 0), axis=0, keepdims=True)
        metav[l] = blank + jnp.sum(jnp.where(hit, value, 0), axis=0, keepdims=True)
    to_smem = pltpu.make_async_copy(permv, perms, load_sem.at[6])
    to_smem.start()

    def m_copy(k):
        to = lax.rem(layer + k, nl)
        return remote(metav.at[to], metar.at[layer], ms_sem.at[k], mr_sem.at[k], grid, to)

    def send_m(k, unused):
        m_copy(k).start()
        return unused

    lax.fori_loop(1, nl, send_m, 0)
    metar[layer] = metav[layer]
    to_smem.wait()
    load_a.wait()

    def a_copy(o, k):
        to = lax.rem(layer + k, nl)
        q = lax.rem(x + turn(o), nx)
        return remote(asend.at[to * nx + q], arecv.at[layer, q], as_sem.at[o, k], ar_sem.at[o, k], grid, to)

    def a_phase(o):
        q = lax.rem(x + turn(o), nx)

        def send_a(k, unused):
            to = lax.rem(layer + k, nl)
            for c in range(cap):
                asend[to * nx + q, c] = a_vm[perms[to, 0, q * cap + c]]
            a_copy(o, k).start()
            return unused

        lax.fori_loop(1, nl, send_a, 0)
        for c in range(cap):
            arecv[layer, q, c] = a_vm[perms[layer, 0, q * cap + c]]

    a_phase(0)
    load_p.wait()
    load_s.wait()
    ptw[fine] = jnp.zeros(ptw.shape[1:], ptw.dtype)
    tot[...] = jnp.zeros_like(tot)

    def spread(ref, at, o0, o1, t0, t1, upright_blocks):
        zero = jnp.zeros_like(t0)
        for b in range(3):
            tile = jnp.where(o0 == b, t0, jnp.where(o1 == b, t1, zero))
            if upright_blocks:
                ref[at, b * 128 : (b + 1) * 128, :] = tile
            else:
                ref[at, :, b * 128 : (b + 1) * 128] = tile

    def offset(col, g):
        return lax.rem(col - g + 1 + ng, ng)

    def transpose_rows(lo):
        for r in range(4):
            i = lo * 4 + r
            o0, o1 = offset(tabs[2, 0, 2 * i], grid), offset(tabs[2, 0, 2 * i + 1], grid)
            spread(ptw, i, o0, o1, p_own[i, 0].T, p_own[i, 1].T, True)

    slots = nl * cap
    widen_units, group_units = fine // WIDEN, slots // GROUP
    units = widen_units + group_units

    def arrive(o):
        rel = turn(o)

        def a_wait(k, unused):
            a_copy(o, k).wait_recv()
            return unused

        lax.fori_loop(1, nl, a_wait, 0)

        @pl.when(o == 0)
        def _():
            def m_wait(k, unused):
                m_copy(k).wait_recv()
                return unused

            lax.fori_loop(1, nl, m_wait, 0)
            pc_copy(2).wait_recv()
            pc_copy(3).wait_recv()
            tables = pltpu.make_async_copy(metar, meta_s, load_sem.at[2])
            tables.start()
            columns = pltpu.make_async_copy(pcbuf, pcs, load_sem.at[3])
            columns.start()
            tables.wait()
            columns.wait()

        for side, at in ((1, 1), (0, 2)):

            @pl.when(o == at)
            def _():
                def one(c, unused):
                    x_copy(side, 1 - side, c).wait_recv()
                    return unused

                lax.fori_loop(0, early_chunks, one, 0)

        @pl.when(o == 3)
        def _():
            def one(c, unused):
                f_copy(0, c).wait_recv()
                f_copy(1, c).wait_recv()
                return unused

            lax.fori_loop(0, early_chunks, one, 0)

    def widen(rel, lo):
        owner = layer * nx + lax.rem(x + rel, nx)

        def one(r, unused):
            j = lo * WIDEN + r
            o0, o1 = offset(pcs[rel, 0, 2 * j], owner), offset(pcs[rel, 0, 2 * j + 1], owner)
            spread(wide, j, o0, o1, pbuf[rel, j, 0], pbuf[rel, j, 1], False)
            return unused

        lax.fori_loop(0, WIDEN, one, 0)

    def some(rel, u):
        q = lax.rem(x + rel, nx)
        lefts, prods = [], []
        for v in range(GROUP):
            n = u * GROUP + v
            src, k = n // cap, n % cap
            m = meta_s[src, 0, q * cap + k]
            i, j = m // SHIFT, m % SHIFT
            prods.append(jnp.dot(arecv[src, q, k], wide[j], preferred_element_type=jnp.float32).astype(jnp.bfloat16))
            lefts.append(ptw[i])
        acc[...] += jnp.dot(
            jnp.concatenate(lefts, axis=1), jnp.concatenate(prods, axis=0), preferred_element_type=jnp.float32
        )

    def flush(rel):
        q = lax.rem(x + rel, nx)
        for a in range(3):
            for b in range(3):
                tot[a, q + b] += acc[a * 128 : (a + 1) * 128, b * 128 : (b + 1) * 128]

    def unit(n):
        o, w = n // units, n % units
        rel = turn(o)

        @pl.when(w == 0)
        def _():
            arrive(o)

        @pl.when(w < widen_units)
        def _():
            widen(rel, w)

        @pl.when(w == widen_units)
        def _():
            acc[...] = jnp.zeros_like(acc)

        @pl.when(w >= widen_units)
        def _():
            some(rel, w - widen_units)

        @pl.when(w == units - 1)
        def _():
            flush(rel)

    pace = -(-units // late_chunks)

    def step(t, unused):
        p_step(t)

        @pl.when(t < nx)
        def _():
            a_phase(t)

        @pl.when(t <= fine // 4)
        def _():
            transpose_rows(t - 1)

        @pl.when(t >= ready)
        def _():
            o, at = (t - ready) // late_chunks, (t - ready) % late_chunks

            def one(v, unused):
                w = at * pace + v

                @pl.when(w < units)
                def _():
                    unit(o * units + w)

                return unused

            lax.fori_loop(0, pace, one, 0)

        return unused

    lax.fori_loop(1, ready + nx * late_chunks, step, 0)

    bf = jnp.bfloat16
    hsend_i[0] = tot[2, 1 : nx + 1].astype(bf)
    hsend_i[1] = tot[0, 1 : nx + 1].astype(bf)
    hsend_c[0] = tot[1, nx + 1].astype(bf)
    hsend_c[1] = tot[1, 0].astype(bf)
    hsend_c[2] = tot[2, nx + 1].astype(bf)
    hsend_c[3] = tot[2, 0].astype(bf)
    hsend_c[4] = tot[0, nx + 1].astype(bf)
    hsend_c[5] = tot[0, 0].astype(bf)
    copies = [
        remote(hsend_i.at[k], hrecv_i.at[k], hs.at[k], hr.at[k], g, layer) for k, g in enumerate((after, before))
    ]
    to = [(g, l) for g in (grid, after, before) for l in (lafter, lbefore)]
    copies += [
        remote(hsend_c.at[k], hrecv_c.at[k], hs.at[2 + k], hr.at[2 + k], g, l) for k, (g, l) in enumerate(to)
    ]
    for copy in copies:
        copy.start()
    for copy in copies:
        copy.wait_recv()
    for b in range(nx):
        total = tot[1, 1 + b]
        for k in range(2):
            total = total + hrecv_i[k, b].astype(jnp.float32)
        if b == 0:
            for k in (0, 2, 4):
                total = total + hrecv_c[k].astype(jnp.float32)
        if b == nx - 1:
            for k in (1, 3, 5):
                total = total + hrecv_c[k].astype(jnp.float32)
        out_ref[0, b] = total.astype(bf)

    for copy in copies:
        copy.wait_send()

    def a_sent(k, unused):
        for o in range(nx):
            a_copy(o, k).wait_send()
        m_copy(k).wait_send()
        return unused

    lax.fori_loop(1, nl, a_sent, 0)

    for s in (0, 1):
        hop = d if s == 0 else lax.rem(nz - d, nz)

        def z_sent(c, unused):
            z_copy(s, c).wait_send()
            return unused

        @pl.when(hop < nz - 1)
        def _():
            lax.fori_loop(0, chunks, z_sent, 0)

        def x_sent(c, unused):
            x_copy(0, s, c).wait_send()
            x_copy(1, s, c).wait_send()
            f_copy(s, c).wait_send()
            return unused

        lax.fori_loop(0, early_chunks, x_sent, 0)

    @pl.when(d < nz - 1)
    def _():
        pc_copy(0).wait_send()

    @pl.when(d == 0)
    def _():
        for s in (0, 1):
            r_copy(0, s).wait_send()
            r_copy(1, s).wait_send()
            g_copy(s).wait_send()

    for which in (1, 2, 3):
        pc_copy(which).wait_send()


def local(nx, a_tiles, a_cols, p_tiles, p_cols):
    fine, per_layer, size, unused = a_tiles.shape
    nl, ng = lax.axis_size("layer"), lax.axis_size("grid")
    nz = ng // nx
    slot_total = fine * per_layer
    cap = 2 * slot_total // ng
    anywhere = pl.BlockSpec(memory_space=pl.ANY)
    flat = a_cols.reshape(1, slot_total)
    rows = lax.broadcasted_iota(jnp.int32, (1, slot_total), 1) // per_layer
    tab = jnp.stack(
        [
            jnp.pad(flat // fine, ((0, 0), (0, 128 - slot_total)), constant_values=4096),
            jnp.pad(rows * SHIFT + flat % fine, ((0, 0), (0, 128 - slot_total))),
            jnp.pad(p_cols.reshape(1, -1), ((0, 0), (0, 128 - 2 * fine))),
        ]
    )
    half = fine // 2
    early_chunks = (half - PLANE_ROWS // 2) // CHUNK
    chunks = early_chunks + nx * (PLANE_ROWS // 2 // CHUNK)
    bf, f32, i32 = jnp.bfloat16, jnp.float32, jnp.int32
    dma = pltpu.SemaphoreType.DMA
    return pl.pallas_call(
        functools.partial(main_kernel, nz, nx, nl, cap, per_layer),
        out_shape=jax.ShapeDtypeStruct((1, nx, size, size), bf),
        in_specs=[anywhere, anywhere, anywhere],
        out_specs=pl.BlockSpec(memory_space=pltpu.VMEM),
        scratch_shapes=[
            pltpu.VMEM((3, 1, 128), i32),
            pltpu.SMEM((3, 1, 128), i32),
            pltpu.VMEM((nl, 1, 128), i32),
            pltpu.SMEM((nl, 1, 128), i32),
            pltpu.VMEM((slot_total, size, size), bf),
            pltpu.VMEM(p_tiles.shape, bf),
            pltpu.VMEM((ng, cap, size, size), bf),
            pltpu.VMEM((nl, nx, cap, size, size), bf),
            pltpu.VMEM((nl, 1, 128), i32),
            pltpu.VMEM((nl, 1, 128), i32),
            pltpu.SMEM((nl, 1, 128), i32),
            pltpu.VMEM((nx,) + p_tiles.shape, bf),
            pltpu.VMEM((nx, 1, 128), i32),
            pltpu.SMEM((nx, 1, 128), i32),
            pltpu.VMEM((fine + 1, 3 * size, size), bf),
            pltpu.VMEM((fine, size, 3 * size), bf),
            pltpu.VMEM((3 * size, 3 * size), f32),
            pltpu.VMEM((3, nx + 2, size, size), f32),
            pltpu.VMEM((2, nx, size, size), bf),
            pltpu.VMEM((6, size, size), bf),
            pltpu.VMEM((2, nx, size, size), bf),
            pltpu.VMEM((6, size, size), bf),
            dma((7,)),
            dma((nx, nl)), dma((nx, nl)), dma((nl,)), dma((nl,)),
            dma((2, chunks)), dma((2, chunks)),
            dma((2, 2, early_chunks)), dma((2, 2, early_chunks)),
            dma((2, early_chunks)), dma((2, early_chunks)),
            dma((2, 2)), dma((2, 2)), dma((2,)), dma((2,)),
            dma((4,)), dma((4,)),
            dma((8,)), dma((8,)),
        ],
        compiler_params=pltpu.CompilerParams(
            collective_id=0, has_side_effects=True, vmem_limit_bytes=58 * 1024 * 1024
        ),
    )(tab, a_tiles.reshape(slot_total, size, size), p_tiles)


def solution(mesh):
    nx = 4
    return jax.shard_map(
        functools.partial(local, nx),
        mesh=mesh,
        in_specs=(
            P("grid", "layer", None, None),
            P("grid", "layer"),
            P("grid", None, None, None),
            P("grid", None),
        ),
        out_specs=P("grid", "layer", None, None),
        check_vma=False,
    )
```

time: 189 us -> 142 us (0.75)
  the two profiles are of different devices: /device:TPU:41 before, /device:TPU:1 now
where the time goes in v2:
time: 142 us
  Pallas kernels  136 us (96%)
  local copies, waits for them, and re-layouts  3.14 us (2%)
  other arithmetic  1.95 us (1%)
    pallas_call x1, Pallas kernels, local(): pl.pallas_call(functools.partial(main_kernel, nz, nx, nl, cap, per_layer)...  136 us

profile of v2, /device:TPU:1, one launch (start us, length us, event | category | flops | bytes accessed | tf_op | source)
XLA Modules:
  0.0 141.5 jit_solution(3220295182051506225)
XLA Ops:
  0.0 0.7 sign_compare_fusion
  0.7 0.7 broadcast_divide_fusion
  1.4 0.1 copy.9
  1.5 0.1 ne.82
  1.6 0.1 copy.11
  1.7 0.1 div.22
  1.8 0.1 copy.10
  1.9 0.1 rem.36
  2.1 0.8 copy.12
  2.9 0.1 reshape.159
  3.0 0.6 pad_add_fusion.tab
  3.6 136.4 %shard_map.46 = bf16[1,4,128,128]{3,2,1,0:T(8,128)(2,1)} custom-call(s32[3,1,128]{2,1,0:T(1,128)} %pad_add_fusion.tab, bf16[96,128,128]{2,1,0:T(8,128)(2,1)} %bitcast.7, bf16[48,2,128,128]{3,2,1,0:T(8,128)(2,1)} %p_hbm.1), custom_call_target="tpu_custom_call" | custom-call | tf_op jit(solution)/shard_map/pallas_call | solution.py:516
  139.9 1.6 %copy.14 = bf16[1,4,128,128]{3,2,1,0:T(8,128)(2,1)} copy(bf16[1,4,128,128]{3,2,1,0:T(8,128)(2,1)} %shard_map.46) | data formatting | bytes 262144
  (3 shorter events, 0.0 us)

commit v3 on v2

v3 whole, which is shorter than its diff:
```python
import functools

import jax
import jax.numpy as jnp
from jax import lax
from jax.experimental import pallas as pl
from jax.experimental.pallas import tpu as pltpu
from jax.sharding import PartitionSpec as P

MESH = pl.DeviceIdType.MESH
SHIFT = 64
CHUNK = 1
XCHUNKS = 1
HOP = 5
LAG = 4
PASS = 8
PLANE_ROWS = 12
GROUP = 16


def main_kernel(
    nz, nx, nl, cap, per_layer,
    tab, a_hbm, p_hbm, out_ref,
    tabv, tabs, permv, perms, a_vm, p_own, asend, arecv, metav, metar, meta_s, zbuf, xbuf, fbuf, pcbuf, pcs, ptw, wide,
    acc, tot, hsend_i, hsend_c, hrecv_i, hrecv_c,
    load_sem, as_sem, ar_sem, m_sem, zs, zr, xs, xr, fs, fr, rs, rr, gs, gr, pcss, pcr, hs, hr,
):
    half = p_own.shape[1] * CHUNK
    fine = 2 * half
    late_chunks = PLANE_ROWS // 2 // CHUNK
    early_chunks = half // CHUNK - late_chunks
    chunks = early_chunks + nx * late_chunks
    ng = nz * nx
    layer = lax.axis_index("layer")
    grid = lax.axis_index("grid")
    z, x = grid // nx, grid % nx
    d = lax.rem(z - layer + nz, nz)
    up = lax.rem(z + 1, nz) * nx + x
    down = lax.rem(z + nz - 1, nz) * nx + x
    right = z * nx + lax.rem(x + 1, nx)
    left = z * nx + lax.rem(x + nx - 1, nx)
    after, before = lax.rem(grid + 1, ng), lax.rem(grid + ng - 1, ng)
    lafter, lbefore = lax.rem(layer + 1, nl), lax.rem(layer + nl - 1, nl)

    def remote(src, dst, ssem, rsem, g, l):
        return pltpu.make_async_remote_copy(
            src_ref=src, dst_ref=dst, send_sem=ssem, recv_sem=rsem, device_id=(g, l), device_id_type=MESH
        )

    def turn(o):
        return o + o // 2 * (1 - 2 * (o % 2))

    load_p = pltpu.make_async_copy(p_hbm, p_own, load_sem.at[1])
    load_a = pltpu.make_async_copy(a_hbm, a_vm, load_sem.at[0])
    load_t = pltpu.make_async_copy(tab, tabv, load_sem.at[2])
    load_s = pltpu.make_async_copy(tab, tabs, load_sem.at[3])
    own_chunks = early_chunks + late_chunks
    first = [
        pltpu.make_async_copy(
            p_hbm.at[s],
            zbuf.at[s, pl.ds(0, own_chunks)],
            load_sem.at[4 + s],
        )
        for s in (0, 1)
    ]
    cols = pltpu.make_async_copy(tab.at[1], pcbuf.at[0], load_sem.at[6])

    @pl.when(d == 0)
    def _():
        for s in (0, 1):
            first[s].start()
        cols.start()

    load_t.start()
    load_s.start()
    load_a.start()
    load_p.start()

    barrier = pltpu.get_barrier_semaphore()
    partners = [(up, layer), (down, layer), (right, layer), (left, layer)]
    partners += [(grid, lax.rem(layer + k, nl)) for k in range(1, nl)]
    partners += [(g, l) for g in (after, before) for l in (layer, lafter, lbefore)]
    for g, l in partners:
        pl.semaphore_signal(barrier, inc=1, device_id=(g, l), device_id_type=MESH)
    pl.semaphore_wait(barrier, len(partners))

    @pl.when(d == 0)
    def _():
        for s in (0, 1):
            first[s].wait()
        cols.wait()

    def late(o):
        return pl.ds(early_chunks + o * late_chunks, late_chunks)

    def z_copy(s, c):
        return remote(zbuf.at[s, c], zbuf.at[s, c], zs.at[s], zr.at[s, c], (up, down)[s], layer)

    def x_copy(side, s, at, count):
        return remote(
            zbuf.at[s, pl.ds(at, count)], xbuf.at[side, s, pl.ds(at, count)], xs.at[side, s], xr.at[side, s],
            (right, left)[side], layer,
        )

    def x_all(side, s):
        return x_copy(side, s, 0, early_chunks)

    def f_copy(s):
        return remote(xbuf.at[s, s], fbuf.at[s], fs.at[s], fr.at[s], (right, left)[s], layer)

    def r_copy(side, s):
        return remote(
            zbuf.at[s, late(0)], zbuf.at[s, late(2 - side)], rs.at[side, s], rr.at[side, s], (right, left)[side], layer
        )

    def g_copy(s):
        return remote(zbuf.at[s, late(2 - s)], zbuf.at[s, late(3)], gs.at[s], gr.at[s], (right, left)[s], layer)

    def pc_copy(which):
        src, dst, g = ((0, 0, up), (0, 3, right), (0, 1, left), (3, 2, right))[which]
        return remote(pcbuf.at[src], pcbuf.at[dst], pcss.at[which], pcr.at[which], g, layer)

    hops = (d, lax.rem(nz - d, nz))
    near, far = jnp.minimum(*hops), jnp.maximum(*hops)
    near_turn = HOP * near
    far_turn = jnp.maximum(near_turn + early_chunks, HOP * far)
    up_first = jnp.minimum(jnp.maximum(hops[1] - hops[0] + 1, 0), 1)
    x_turn = (
        up_first * near_turn + (1 - up_first) * far_turn,
        up_first * far_turn + (1 - up_first) * near_turn,
    )
    pass_turn = jnp.maximum(far_turn + early_chunks + LAG, chunks + PASS)
    ready = jnp.maximum(early_chunks + late_chunks + HOP * far, pass_turn + 1 - late_chunks)

    def p_step(t):
        for s in (0, 1):
            hop = hops[s]
            c = t - HOP * hop

            @pl.when((c >= 0) & (c < chunks))
            def _():
                @pl.when(d != 0)
                def _():
                    z_copy(s, c).wait_recv()

                @pl.when(d == 0)
                def _():
                    @pl.when(c == early_chunks + (1 + s) * late_chunks)
                    def _():
                        r_copy(1 - s, s).wait_recv()

                    @pl.when(c == early_chunks + 3 * late_chunks)
                    def _():
                        g_copy(s).wait_recv()

                @pl.when(hop < nz - 1)
                def _():
                    z_copy(s, c).start()

                if s == 0:

                    @pl.when(c == 0)
                    def _():
                        @pl.when(d != 0)
                        def _():
                            pc_copy(0).wait_recv()

                        @pl.when(hop < nz - 1)
                        def _():
                            pc_copy(0).start()

                        pc_copy(1).start()
                        pc_copy(2).start()

                    @pl.when(c == 2)
                    def _():
                        pc_copy(1).wait_recv()
                        pc_copy(3).start()

                @pl.when((d == 0) & (c == 0))
                def _():
                    r_copy(0, s).start()
                    r_copy(1, s).start()

                @pl.when((d == 0) & (c == early_chunks))
                def _():
                    r_copy(s, s).wait_recv()
                    g_copy(s).start()

            e = t - x_turn[s]

            @pl.when((e >= 0) & (e < early_chunks) & (lax.rem(e + XCHUNKS, XCHUNKS) == XCHUNKS - 1))
            def _():
                x_copy(0, s, e - (XCHUNKS - 1), XCHUNKS).start()
                x_copy(1, s, e - (XCHUNKS - 1), XCHUNKS).start()

        @pl.when(t == pass_turn)
        def _():
            for s in (0, 1):
                x_all(s, s).wait_recv()
                f_copy(s).start()

    p_step(0)

    load_t.wait()
    size = tabv.shape[2]
    per = nx * cap
    blank = fine * SHIFT
    rows = lax.broadcasted_iota(jnp.int32, (size, size), 0)
    lanes = lax.broadcasted_iota(jnp.int32, (size, size), 1)

    def upright(v):
        return jnp.broadcast_to(v, (size, size)).T

    def count_steps(v, width, most):
        total = jnp.zeros_like(v)
        for k in range(1, most):
            total = total + jnp.where(v >= k * width, 1, 0)
        return total

    col, lane = tabv[0], lanes[0:1]
    owner_of = count_steps(col, fine, ng)
    own = jnp.where(lane < a_vm.shape[0], owner_of, SHIFT * ng)
    packed = count_steps(lane, per_layer, fine) * SHIFT + col - owner_of * fine
    same = (upright(own) == jnp.broadcast_to(own, (size, size))) & (rows < lanes)
    rank = jnp.sum(jnp.where(same, 1, 0), axis=0, keepdims=True)
    slot = upright(own * cap + rank)
    value = upright(packed - blank)
    for l in range(nl):
        hit = (slot == l * per + lanes) & (lanes < per) & (rows < a_vm.shape[0])
        permv[l] = jnp.sum(jnp.where(hit, rows, 0), axis=0, keepdims=True)
        metav[l] = blank + jnp.sum(jnp.where(hit, value, 0), axis=0, keepdims=True)
    to_smem = pltpu.make_async_copy(permv, perms, load_sem.at[7])
    to_smem.start()

    def m_copy(k):
        to = lax.rem(layer + k, nl)
        return remote(metav.at[to], metar.at[layer], m_sem.at[0], m_sem.at[1], grid, to)

    m_all = remote(metav.at[pl.ds(0, nl - 1)], metar.at[pl.ds(0, nl - 1)], m_sem.at[0], m_sem.at[1], grid, lafter)
    for k in range(1, nl):
        m_copy(k).start()
    metar[layer] = metav[layer]
    to_smem.wait()
    load_a.wait()

    def a_copy(o, k):
        to = lax.rem(layer + k, nl)
        return remote(asend.at[o * nl + k], arecv.at[o, layer], as_sem.at[o], ar_sem.at[o], grid, to)

    def a_all(o):
        part = pl.ds(0, nl - 1)
        return remote(asend.at[part], arecv.at[o, part], as_sem.at[o], ar_sem.at[o], grid, lafter)

    def a_phase(o):
        q = lax.rem(x + turn(o), nx)

        def send_a(k, unused):
            to = lax.rem(layer + k, nl)
            for c in range(cap):
                asend[o * nl + k, c] = a_vm[perms[to, 0, q * cap + c]]
            a_copy(o, k).start()
            return unused

        lax.fori_loop(1, nl, send_a, 0)
        for c in range(cap):
            arecv[o, layer, c] = a_vm[perms[layer, 0, q * cap + c]]

    a_phase(0)
    load_p.wait()
    load_s.wait()
    ptw[fine] = jnp.zeros(ptw.shape[1:], ptw.dtype)
    tot[...] = jnp.zeros_like(tot)

    def spread(ref, at, o0, o1, t0, t1, upright_blocks):
        zero = jnp.zeros_like(t0)
        for b in range(3):
            tile = jnp.where(o0 == b, t0, jnp.where(o1 == b, t1, zero))
            if upright_blocks:
                ref[at, b * 128 : (b + 1) * 128, :] = tile
            else:
                ref[at, :, b * 128 : (b + 1) * 128] = tile

    def offset(col, g):
        return lax.rem(col - g + 1 + ng, ng)

    def transpose_rows(lo):
        for r in range(4):
            i = lo * 4 + r
            o0, o1 = offset(tabs[1, 0, 2 * i], grid), offset(tabs[1, 0, 2 * i + 1], grid)
            s, c = lax.div(i, half), lax.div(lax.rem(i, half), CHUNK)
            at = (s, c, lax.rem(i, CHUNK))
            spread(ptw, i, o0, o1, p_own[at + (0,)].T, p_own[at + (1,)].T, True)

    slots = nl * cap
    widen_units, group_units = 4, slots // GROUP
    units = widen_units + group_units

    def arrive(o):
        a_all(o).wait_recv()

        @pl.when(o == 0)
        def _():
            m_all.wait_recv()
            pc_copy(2).wait_recv()
            pc_copy(3).wait_recv()
            tables = pltpu.make_async_copy(metar, meta_s, load_sem.at[2])
            tables.start()
            columns = pltpu.make_async_copy(pcbuf, pcs, load_sem.at[3])
            columns.start()
            tables.wait()
            columns.wait()

        @pl.when(o == 1)
        def _():
            x_all(1, 0).wait_recv()

        @pl.when(o == 2)
        def _():
            x_all(0, 1).wait_recv()

        @pl.when(o == 3)
        def _():
            f_copy(0).wait_recv()
            f_copy(1).wait_recv()

    def widen(o, w):
        rel = turn(o)
        owner = layer * nx + lax.rem(x + rel, nx)
        for s in (0, 1):

            def widen_row(ref, at, c, r, start):
                j = s * half + start + c * CHUNK + r
                o0, o1 = offset(pcs[rel, 0, 2 * j], owner), offset(pcs[rel, 0, 2 * j + 1], owner)
                spread(wide, j, o0, o1, ref[at + (c, r, 0)], ref[at + (c, r, 1)], False)

            for turn_of, (ref, at) in enumerate(
                ((zbuf, (s,)), (xbuf, (1, s)), (xbuf, (0, s)), (fbuf, (s,)))
            ):

                @pl.when((w == 2 * s) & (o == turn_of))
                def _():
                    def one(c, unused):
                        for r in range(CHUNK):
                            widen_row(ref, at, c, r, 0)
                        return unused

                    lax.fori_loop(0, early_chunks, one, 0)

            @pl.when(w == 2 * s + 1)
            def _():
                def one(c, unused):
                    j = s * half + early_chunks * CHUNK + c * CHUNK
                    for r in range(CHUNK):
                        o0 = offset(pcs[rel, 0, 2 * (j + r)], owner)
                        o1 = offset(pcs[rel, 0, 2 * (j + r) + 1], owner)
                        at = early_chunks + o * late_chunks + c
                        spread(wide, j + r, o0, o1, zbuf[s, at, r, 0], zbuf[s, at, r, 1], False)
                    return unused

                lax.fori_loop(0, late_chunks, one, 0)

    def some(o, u):
        q = lax.rem(x + turn(o), nx)
        lefts, prods = [], []
        for v in range(GROUP):
            n = u * GROUP + v
            src = lax.div(n, cap)
            k = n - src * cap
            m = meta_s[src, 0, q * cap + k]
            i, j = m // SHIFT, m % SHIFT
            prods.append(jnp.dot(arecv[o, src, k], wide[j], preferred_element_type=jnp.float32).astype(jnp.bfloat16))
            lefts.append(ptw[i])
        acc[...] += jnp.dot(
            jnp.concatenate(lefts, axis=1), jnp.concatenate(prods, axis=0), preferred_element_type=jnp.float32
        )

    def flush(o):
        q = lax.rem(x + turn(o), nx)
        for a in range(3):
            for b in range(3):
                tot[a, q + b] += acc[a * 128 : (a + 1) * 128, b * 128 : (b + 1) * 128]

    def unit(o, w):
        @pl.when(w == 0)
        def _():
            arrive(o)
            acc[...] = jnp.zeros_like(acc)

        @pl.when(w < widen_units)
        def _():
            widen(o, w)

        @pl.when(w >= widen_units)
        def _():
            some(o, w - widen_units)

        @pl.when(w == units - 1)
        def _():
            flush(o)

    pace = -(-units // late_chunks)

    def step(t, unused):
        p_step(t)

        @pl.when(t < nx)
        def _():
            a_phase(t)

        @pl.when(t <= fine // 4)
        def _():
            transpose_rows(t - 1)

        @pl.when(t >= ready)
        def _():
            o = lax.div(t - ready, late_chunks)
            at = t - ready - o * late_chunks

            def one(v, unused):
                w = at * pace + v

                @pl.when(w < units)
                def _():
                    unit(o, w)

                return unused

            lax.fori_loop(0, pace, one, 0)

        return unused

    lax.fori_loop(1, ready + nx * late_chunks, step, 0)

    for o in range(nx):
        a_all(o).wait_send()
    m_all.wait_send()
    for s in (0, 1):

        @pl.when(hops[s] < nz - 1)
        def _():
            remote(zbuf.at[s], zbuf.at[s], zs.at[s], zr.at[s, 0], (up, down)[s], layer).wait_send()

        x_all(0, s).wait_send()
        x_all(1, s).wait_send()
        f_copy(s).wait_send()

        @pl.when(d == 0)
        def _():
            r_copy(0, s).wait_send()
            r_copy(1, s).wait_send()
            g_copy(s).wait_send()

    @pl.when(d < nz - 1)
    def _():
        pc_copy(0).wait_send()

    for which in (1, 2, 3):
        pc_copy(which).wait_send()

    bf = jnp.bfloat16
    hsend_i[0] = tot[2, 1 : nx + 1].astype(bf)
    hsend_i[1] = tot[0, 1 : nx + 1].astype(bf)
    hsend_c[0] = tot[1, nx + 1].astype(bf)
    hsend_c[1] = tot[1, 0].astype(bf)
    hsend_c[2] = tot[2, nx + 1].astype(bf)
    hsend_c[3] = tot[2, 0].astype(bf)
    hsend_c[4] = tot[0, nx + 1].astype(bf)
    hsend_c[5] = tot[0, 0].astype(bf)
    copies = [
        remote(hsend_i.at[k], hrecv_i.at[k], hs.at[k], hr.at[k], g, layer) for k, g in enumerate((after, before))
    ]
    to = [(g, l) for g in (grid, after, before) for l in (lafter, lbefore)]
    copies += [
        remote(hsend_c.at[k], hrecv_c.at[k], hs.at[2 + k], hr.at[2 + k], g, l) for k, (g, l) in enumerate(to)
    ]
    for copy in copies:
        copy.start()
    for copy in copies:
        copy.wait_recv()
    for b in range(nx):
        total = tot[1, 1 + b]
        for k in range(2):
            total = total + hrecv_i[k, b].astype(jnp.float32)
        if b == 0:
            for k in (0, 2, 4):
                total = total + hrecv_c[k].astype(jnp.float32)
        if b == nx - 1:
            for k in (1, 3, 5):
                total = total + hrecv_c[k].astype(jnp.float32)
        out_ref[0, b] = total.astype(bf)

    for copy in copies:
        copy.wait_send()


def local(nx, a_tiles, a_cols, p_tiles, p_cols):
    fine, per_layer, size, unused = a_tiles.shape
    nl, ng = lax.axis_size("layer"), lax.axis_size("grid")
    nz = ng // nx
    slot_total = fine * per_layer
    cap = 2 * slot_total // ng
    anywhere = pl.BlockSpec(memory_space=pl.ANY)
    def lane_row(v):
        v = v.reshape(1, 1, -1)
        return jnp.pad(v, ((0, 0), (0, 0), (0, 128 - v.shape[2])))

    tab = jnp.concatenate([lane_row(a_cols), lane_row(p_cols)])
    half = fine // 2
    early_chunks = (half - PLANE_ROWS // 2) // CHUNK
    chunks = early_chunks + nx * (PLANE_ROWS // 2 // CHUNK)
    row = p_tiles.shape[1:]
    bf, f32, i32 = jnp.bfloat16, jnp.float32, jnp.int32
    dma = pltpu.SemaphoreType.DMA
    return pl.pallas_call(
        functools.partial(main_kernel, nz, nx, nl, cap, per_layer),
        out_shape=jax.ShapeDtypeStruct((1, nx, size, size), bf),
        in_specs=[anywhere, anywhere, anywhere],
        out_specs=pl.BlockSpec(memory_space=pltpu.VMEM),
        scratch_shapes=[
            pltpu.VMEM((2, 1, 128), i32),
            pltpu.SMEM((2, 1, 128), i32),
            pltpu.VMEM((nl, 1, 128), i32),
            pltpu.SMEM((nl, 1, 128), i32),
            pltpu.VMEM((slot_total, size, size), bf),
            pltpu.VMEM((2, early_chunks + PLANE_ROWS // 2 // CHUNK, CHUNK) + row, bf),
            pltpu.VMEM((ng, cap, size, size), bf),
            pltpu.VMEM((nx, nl, cap, size, size), bf),
            pltpu.VMEM((nl, 1, 128), i32),
            pltpu.VMEM((nl, 1, 128), i32),
            pltpu.SMEM((nl, 1, 128), i32),
            pltpu.VMEM((2, chunks, CHUNK) + row, bf),
            pltpu.VMEM((2, 2, early_chunks, CHUNK) + row, bf),
            pltpu.VMEM((2, early_chunks, CHUNK) + row, bf),
            pltpu.VMEM((nx, 1, 128), i32),
            pltpu.SMEM((nx, 1, 128), i32),
            pltpu.VMEM((fine + 1, 3 * size, size), bf),
            pltpu.VMEM((fine, size, 3 * size), bf),
            pltpu.VMEM((3 * size, 3 * size), f32),
            pltpu.VMEM((3, nx + 2, size, size), f32),
            pltpu.VMEM((2, nx, size, size), bf),
            pltpu.VMEM((6, size, size), bf),
            pltpu.VMEM((2, nx, size, size), bf),
            pltpu.VMEM((6, size, size), bf),
            dma((8,)),
            dma((nx,)), dma((nx,)), dma((2,)),
            dma((2,)), dma((2, chunks)),
            dma((2, 2)), dma((2, 2)),
            dma((2,)), dma((2,)),
            dma((2, 2)), dma((2, 2)), dma((2,)), dma((2,)),
            dma((4,)), dma((4,)),
            dma((8,)), dma((8,)),
        ],
        compiler_params=pltpu.CompilerParams(
            collective_id=0, has_side_effects=True, vmem_limit_bytes=58 * 1024 * 1024
        ),
    )(tab, a_tiles.reshape(slot_total, size, size), p_tiles.reshape((2, early_chunks + PLANE_ROWS // 2 // CHUNK, CHUNK) + row))


def solution(mesh):
    nx = 4
    return jax.shard_map(
        functools.partial(local, nx),
        mesh=mesh,
        in_specs=(
            P("grid", "layer", None, None),
            P("grid", "layer"),
            P("grid", None, None, None),
            P("grid", None),
        ),
        out_specs=P("grid", "layer", None, None),
        check_vma=False,
    )
```

time: 142 us -> 126 us (0.89)
  Pallas kernels: 136 us -> 120 us
    pallas_call x1, Pallas kernels: 136 us -> 120 us  [local(): pl.pallas_call(functools.partial(main_kernel, nz, nx, nl, cap, per_layer)...]
    unnamed x2 -> x3, local copies, waits for them, and re-layouts: 2.34 us -> 3.1 us
where the time goes in v3:
time: 126 us; the launch traced here: 124 us
  Pallas kernels  120 us (95%)
  local copies, waits for them, and re-layouts  3.34 us (3%)
    pallas_call x1, Pallas kernels, local(): pl.pallas_call(functools.partial(main_kernel, nz, nx, nl, cap, per_layer)...  120 us
    unnamed x3, local copies, waits for them, and re-layouts  3.1 us

profile of v3, /device:TPU:1, one launch (start us, length us, event | category | flops | bytes accessed | tf_op | source)
XLA Modules:
  0.0 124.3 jit_solution(8189711944139318886)
XLA Ops:
  0.0 0.8 copy.7
  0.8 0.1 reshape.12
  0.9 0.8 copy.8
  1.7 0.1 reshape.13
  1.8 0.6 pad_add_fusion.tab
  2.3 120.4 %shard_map.46 = bf16[1,4,128,128]{3,2,1,0:T(8,128)(2,1)} custom-call(s32[2,1,128]{2,1,0:T(1,128)} %pad_add_fusion.tab, bf16[96,128,128]{2,1,0:T(8,128)(2,1)} %bitcast.2, bf16[2,24,1,2,128,128]{5,4,3,2,1,0:T(8,128)(2,1)} %bitcast.3), custom_call_target="tpu_custom_call" | custom-call | tf_op jit(solution)/shard_map/pallas_call | solution.py:515
  122.7 1.6 %copy.10 = bf16[1,4,128,128]{3,2,1,0:T(8,128)(2,1)} copy(bf16[1,4,128,128]{3,2,1,0:T(8,128)(2,1)} %shard_map.46) | data formatting | bytes 262144

commit v4 on v3

--- a/solution.py
+++ b/solution.py
@@ -10,12 +10,12 @@
 MESH = pl.DeviceIdType.MESH
 SHIFT = 64
 CHUNK = 1
-XCHUNKS = 1
-HOP = 5
-LAG = 4
-PASS = 8
+PARTS = 3
+SPACING = 10
+HOP = 4
+LAG = 3
 PLANE_ROWS = 12
-GROUP = 16
+GROUP = 24
 
 
 def main_kernel(
@@ -23,7 +23,7 @@
     tab, a_hbm, p_hbm, out_ref,
     tabv, tabs, permv, perms, a_vm, p_own, asend, arecv, metav, metar, meta_s, zbuf, xbuf, fbuf, pcbuf, pcs, ptw, wide,
     acc, tot, hsend_i, hsend_c, hrecv_i, hrecv_c,
-    load_sem, as_sem, ar_sem, m_sem, zs, zr, xs, xr, fs, fr, rs, rr, gs, gr, pcss, pcr, hs, hr,
+    load_sem, as_sem, ar_sem, m_sem, zs, zr, xs, xr, fs, fr, rs, rr, pcss, pcr, hs, hr,
 ):
     half = p_own.shape[1] * CHUNK
     fine = 2 * half
@@ -63,7 +63,7 @@
         )
         for s in (0, 1)
     ]
-    cols = pltpu.make_async_copy(tab.at[1], pcbuf.at[0], load_sem.at[6])
+    cols = pltpu.make_async_copy(tab.at[pl.ds(2, 2)], pcbuf.at[0], load_sem.at[6])
 
     @pl.when(d == 0)
     def _():
@@ -82,7 +82,17 @@
     partners += [(g, l) for g in (after, before) for l in (layer, lafter, lbefore)]
     for g, l in partners:
         pl.semaphore_signal(barrier, inc=1, device_id=(g, l), device_id_type=MESH)
-    pl.semaphore_wait(barrier, len(partners))
+
+    @pl.when(d == 0)
+    def _():
+        for k in range(1, nx):
+            for y in range(nl // 2):
+                pl.semaphore_signal(
+                    barrier, inc=1, device_id=(z * nx + lax.rem(x + k, nx), 2 * y + lax.rem(z, 2)), device_id_type=MESH
+                )
+
+    pl.semaphore_wait(barrier, len(partners) + (nx - 1) * (1 - lax.rem(layer + z, 2)))
+
 
     @pl.when(d == 0)
     def _():
@@ -96,25 +106,46 @@
     def z_copy(s, c):
         return remote(zbuf.at[s, c], zbuf.at[s, c], zs.at[s], zr.at[s, c], (up, down)[s], layer)
 
+    part = early_chunks // PARTS
+
     def x_copy(side, s, at, count):
         return remote(
-            zbuf.at[s, pl.ds(at, count)], xbuf.at[side, s, pl.ds(at, count)], xs.at[side, s], xr.at[side, s],
-            (right, left)[side], layer,
+            zbuf.at[s, pl.ds(at, count)], xbuf.at[side, s, pl.ds(at, count)],
+            xs.at[side, s], xr.at[side, s, lax.div(at, part)], (right, left)[side], layer,
         )
 
-    def x_all(side, s):
+    def x_part(side, s, p):
+        return x_copy(side, s, p * part, part)
+
+    def x_sent(side, s):
         return x_copy(side, s, 0, early_chunks)
 
-    def f_copy(s):
-        return remote(xbuf.at[s, s], fbuf.at[s], fs.at[s], fr.at[s], (right, left)[s], layer)
-
-    def r_copy(side, s):
+    def f_copy(s, at, count):
         return remote(
-            zbuf.at[s, late(0)], zbuf.at[s, late(2 - side)], rs.at[side, s], rr.at[side, s], (right, left)[side], layer
+            xbuf.at[s, s, pl.ds(at, count)], fbuf.at[s, pl.ds(at, count)], fs.at[s], fr.at[s], (right, left)[s], layer
         )
 
-    def g_copy(s):
-        return remote(zbuf.at[s, late(2 - s)], zbuf.at[s, late(3)], gs.at[s], gr.at[s], (right, left)[s], layer)
+    def f_all(s):
+        return f_copy(s, 0, early_chunks)
+
+    planes = nl // 2
+    shares = 4 // planes
+    part_chunks = late_chunks // 2
+    opposite = z * nx + lax.rem(x + 2, nx)
+    sends_late = lax.rem(layer, 2) == lax.rem(z, 2)
+
+    def r_copy(k, u):
+        o, g = ((2, right), (1, left), (3, opposite))[k]
+        at = lax.div(layer, 2) * shares + u
+        s = lax.div(at, 2)
+        start = early_chunks + (at - 2 * s) * part_chunks
+        return remote(
+            p_own.at[s, pl.ds(start, part_chunks)], zbuf.at[s, pl.ds(start + o * late_chunks, part_chunks)],
+            rs.at[k, u], rr.at[o - 1, s], g, z,
+        )
+
+    def r_all(o, s):
+        return remote(zbuf.at[s, late(o)], zbuf.at[s, late(o)], rs.at[0, 0], rr.at[o - 1, s], right, layer)
 
     def pc_copy(which):
         src, dst, g = ((0, 0, up), (0, 3, right), (0, 1, left), (3, 2, right))[which]
@@ -129,8 +160,9 @@
         up_first * near_turn + (1 - up_first) * far_turn,
         up_first * far_turn + (1 - up_first) * near_turn,
     )
-    pass_turn = jnp.maximum(far_turn + early_chunks + LAG, chunks + PASS)
-    ready = jnp.maximum(early_chunks + late_chunks + HOP * far, pass_turn + 1 - late_chunks)
+    pass_turn = far_turn + early_chunks // PARTS + LAG
+    first_turn = early_chunks + late_chunks + HOP * far
+    rest_turn = jnp.maximum(first_turn + late_chunks, pass_turn + (PARTS - 1) * SPACING + 1)
 
     def p_step(t):
         for s in (0, 1):
@@ -145,13 +177,11 @@
 
                 @pl.when(d == 0)
                 def _():
-                    @pl.when(c == early_chunks + (1 + s) * late_chunks)
-                    def _():
-                        r_copy(1 - s, s).wait_recv()
-
-                    @pl.when(c == early_chunks + 3 * late_chunks)
-                    def _():
-                        g_copy(s).wait_recv()
+                    for o in range(1, nx):
+
+                        @pl.when(c == early_chunks + o * late_chunks)
+                        def _():
+                            r_all(o, s).wait_recv()
 
                 @pl.when(hop < nz - 1)
                 def _():
@@ -177,28 +207,20 @@
                         pc_copy(1).wait_recv()
                         pc_copy(3).start()
 
-                @pl.when((d == 0) & (c == 0))
-                def _():
-                    r_copy(0, s).start()
-                    r_copy(1, s).start()
-
-                @pl.when((d == 0) & (c == early_chunks))
-                def _():
-                    r_copy(s, s).wait_recv()
-                    g_copy(s).start()
-
             e = t - x_turn[s]
 
-            @pl.when((e >= 0) & (e < early_chunks) & (lax.rem(e + XCHUNKS, XCHUNKS) == XCHUNKS - 1))
+            @pl.when((e >= 0) & (e < early_chunks))
             def _():
-                x_copy(0, s, e - (XCHUNKS - 1), XCHUNKS).start()
-                x_copy(1, s, e - (XCHUNKS - 1), XCHUNKS).start()
-
-        @pl.when(t == pass_turn)
-        def _():
-            for s in (0, 1):
-                x_all(s, s).wait_recv()
-                f_copy(s).start()
+                x_copy(0, s, e, 1).start()
+                x_copy(1, s, e, 1).start()
+
+        for p in range(PARTS):
+
+            @pl.when(t == pass_turn + p * SPACING)
+            def _():
+                for s in (0, 1):
+                    x_part(s, s, p).wait_recv()
+                    f_copy(s, p * part, part).start()
 
     p_step(0)
 
@@ -218,17 +240,21 @@
             total = total + jnp.where(v >= k * width, 1, 0)
         return total
 
-    col, lane = tabv[0], lanes[0:1]
+    lane = lanes[0:1]
+    second = jnp.where(lane >= 64, 1, 0)
+    col = jnp.where(lane >= 64, pltpu.roll(tabv[1], 64, 1), tabv[0])
+    row = lane - 64 * second
+    tile = 2 * rows - 127 * jnp.where(rows >= 64, 1, 0)
     owner_of = count_steps(col, fine, ng)
-    own = jnp.where(lane < a_vm.shape[0], owner_of, SHIFT * ng)
-    packed = count_steps(lane, per_layer, fine) * SHIFT + col - owner_of * fine
+    own = jnp.where(row < fine, owner_of, SHIFT * ng)
+    packed = row * SHIFT + col - owner_of * fine
     same = (upright(own) == jnp.broadcast_to(own, (size, size))) & (rows < lanes)
     rank = jnp.sum(jnp.where(same, 1, 0), axis=0, keepdims=True)
     slot = upright(own * cap + rank)
     value = upright(packed - blank)
     for l in range(nl):
-        hit = (slot == l * per + lanes) & (lanes < per) & (rows < a_vm.shape[0])
-        permv[l] = jnp.sum(jnp.where(hit, rows, 0), axis=0, keepdims=True)
+        hit = (slot == l * per + lanes) & (lanes < per)
+        permv[l] = jnp.sum(jnp.where(hit, tile, 0), axis=0, keepdims=True)
         metav[l] = blank + jnp.sum(jnp.where(hit, value, 0), axis=0, keepdims=True)
     to_smem = pltpu.make_async_copy(permv, perms, load_sem.at[7])
     to_smem.start()
@@ -266,8 +292,15 @@
         for c in range(cap):
             arecv[o, layer, c] = a_vm[perms[layer, 0, q * cap + c]]
 
+    load_p.wait()
+
+    @pl.when(sends_late)
+    def _():
+        for k in range(3):
+            for u in range(shares):
+                r_copy(k, u).start()
+
     a_phase(0)
-    load_p.wait()
     load_s.wait()
     ptw[fine] = jnp.zeros(ptw.shape[1:], ptw.dtype)
     tot[...] = jnp.zeros_like(tot)
@@ -287,7 +320,7 @@
     def transpose_rows(lo):
         for r in range(4):
             i = lo * 4 + r
-            o0, o1 = offset(tabs[1, 0, 2 * i], grid), offset(tabs[1, 0, 2 * i + 1], grid)
+            o0, o1 = offset(tabs[2, 0, i], grid), offset(tabs[3, 0, i], grid)
             s, c = lax.div(i, half), lax.div(lax.rem(i, half), CHUNK)
             at = (s, c, lax.rem(i, CHUNK))
             spread(ptw, i, o0, o1, p_own[at + (0,)].T, p_own[at + (1,)].T, True)
@@ -313,16 +346,18 @@
 
         @pl.when(o == 1)
         def _():
-            x_all(1, 0).wait_recv()
+            for p in range(PARTS):
+                x_part(1, 0, p).wait_recv()
 
         @pl.when(o == 2)
         def _():
-            x_all(0, 1).wait_recv()
+            for p in range(PARTS):
+                x_part(0, 1, p).wait_recv()
 
         @pl.when(o == 3)
         def _():
-            f_copy(0).wait_recv()
-            f_copy(1).wait_recv()
+            f_all(0).wait_recv()
+            f_all(1).wait_recv()
 
     def widen(o, w):
         rel = turn(o)
@@ -331,7 +366,7 @@
 
             def widen_row(ref, at, c, r, start):
                 j = s * half + start + c * CHUNK + r
-                o0, o1 = offset(pcs[rel, 0, 2 * j], owner), offset(pcs[rel, 0, 2 * j + 1], owner)
+                o0, o1 = offset(pcs[rel, 0, 0, j], owner), offset(pcs[rel, 1, 0, j], owner)
                 spread(wide, j, o0, o1, ref[at + (c, r, 0)], ref[at + (c, r, 1)], False)
 
             for turn_of, (ref, at) in enumerate(
@@ -352,8 +387,8 @@
                 def one(c, unused):
                     j = s * half + early_chunks * CHUNK + c * CHUNK
                     for r in range(CHUNK):
-                        o0 = offset(pcs[rel, 0, 2 * (j + r)], owner)
-                        o1 = offset(pcs[rel, 0, 2 * (j + r) + 1], owner)
+                        o0 = offset(pcs[rel, 0, 0, j + r], owner)
+                        o1 = offset(pcs[rel, 1, 0, j + r], owner)
                         at = early_chunks + o * late_chunks + c
                         spread(wide, j + r, o0, o1, zbuf[s, at, r, 0], zbuf[s, at, r, 1], False)
                     return unused
@@ -412,10 +447,12 @@
         def _():
             transpose_rows(t - 1)
 
-        @pl.when(t >= ready)
-        def _():
-            o = lax.div(t - ready, late_chunks)
-            at = t - ready - o * late_chunks
+        @pl.when((t >= first_turn) & ((t < first_turn + late_chunks) | (t >= rest_turn)))
+        def _():
+            rest = jnp.minimum(jnp.maximum(t - rest_turn + 1, 0), 1)
+            since = t - first_turn - rest * (rest_turn - late_chunks - first_turn)
+            o = lax.div(since, late_chunks)
+            at = since - o * late_chunks
 
             def one(v, unused):
                 w = at * pace + v
@@ -430,33 +467,7 @@
 
         return unused
 
-    lax.fori_loop(1, ready + nx * late_chunks, step, 0)
-
-    for o in range(nx):
-        a_all(o).wait_send()
-    m_all.wait_send()
-    for s in (0, 1):
-
-        @pl.when(hops[s] < nz - 1)
-        def _():
-            remote(zbuf.at[s], zbuf.at[s], zs.at[s], zr.at[s, 0], (up, down)[s], layer).wait_send()
-
-        x_all(0, s).wait_send()
-        x_all(1, s).wait_send()
-        f_copy(s).wait_send()
-
-        @pl.when(d == 0)
-        def _():
-            r_copy(0, s).wait_send()
-            r_copy(1, s).wait_send()
-            g_copy(s).wait_send()
-
-    @pl.when(d < nz - 1)
-    def _():
-        pc_copy(0).wait_send()
-
-    for which in (1, 2, 3):
-        pc_copy(which).wait_send()
+    lax.fori_loop(1, rest_turn + (nx - 1) * late_chunks, step, 0)
 
     bf = jnp.bfloat16
     hsend_i[0] = tot[2, 1 : nx + 1].astype(bf)
@@ -476,6 +487,32 @@
     ]
     for copy in copies:
         copy.start()
+    for o in range(nx):
+        a_all(o).wait_send()
+    m_all.wait_send()
+    for s in (0, 1):
+
+        @pl.when(hops[s] < nz - 1)
+        def _():
+            remote(zbuf.at[s], zbuf.at[s], zs.at[s], zr.at[s, 0], (up, down)[s], layer).wait_send()
+
+        x_sent(0, s).wait_send()
+        x_sent(1, s).wait_send()
+        f_all(s).wait_send()
+
+    @pl.when(sends_late)
+    def _():
+        for k in range(3):
+            for u in range(shares):
+                r_copy(k, u).wait_send()
+
+    @pl.when(d < nz - 1)
+    def _():
+        pc_copy(0).wait_send()
+
+    for which in (1, 2, 3):
+        pc_copy(which).wait_send()
+
     for copy in copies:
         copy.wait_recv()
     for b in range(nx):
@@ -501,11 +538,8 @@
     slot_total = fine * per_layer
     cap = 2 * slot_total // ng
     anywhere = pl.BlockSpec(memory_space=pl.ANY)
-    def lane_row(v):
-        v = v.reshape(1, 1, -1)
-        return jnp.pad(v, ((0, 0), (0, 0), (0, 128 - v.shape[2])))
-
-    tab = jnp.concatenate([lane_row(a_cols), lane_row(p_cols)])
+    tab = jnp.concatenate([a_cols.T, p_cols.T])
+    tab = jnp.pad(tab, ((0, 0), (0, 128 - fine))).reshape(2 * per_layer, 1, 128)
     half = fine // 2
     early_chunks = (half - PLANE_ROWS // 2) // CHUNK
     chunks = early_chunks + nx * (PLANE_ROWS // 2 // CHUNK)
@@ -518,8 +552,8 @@
         in_specs=[anywhere, anywhere, anywhere],
         out_specs=pl.BlockSpec(memory_space=pltpu.VMEM),
         scratch_shapes=[
-            pltpu.VMEM((2, 1, 128), i32),
-            pltpu.SMEM((2, 1, 128), i32),
+            pltpu.VMEM((4, 1, 128), i32),
+            pltpu.SMEM((4, 1, 128), i32),
             pltpu.VMEM((nl, 1, 128), i32),
             pltpu.SMEM((nl, 1, 128), i32),
             pltpu.VMEM((slot_total, size, size), bf),
@@ -532,8 +566,8 @@
             pltpu.VMEM((2, chunks, CHUNK) + row, bf),
             pltpu.VMEM((2, 2, early_chunks, CHUNK) + row, bf),
             pltpu.VMEM((2, early_chunks, CHUNK) + row, bf),
-            pltpu.VMEM((nx, 1, 128), i32),
-            pltpu.SMEM((nx, 1, 128), i32),
+            pltpu.VMEM((nx, 2, 1, 128), i32),
+            pltpu.SMEM((nx, 2, 1, 128), i32),
             pltpu.VMEM((fine + 1, 3 * size, size), bf),
             pltpu.VMEM((fine, size, 3 * size), bf),
             pltpu.VMEM((3 * size, 3 * size), f32),
@@ -545,9 +579,9 @@
             dma((8,)),
             dma((nx,)), dma((nx,)), dma((2,)),
             dma((2,)), dma((2, chunks)),
-            dma((2, 2)), dma((2, 2)),
+            dma((2, 2)), dma((2, 2, PARTS)),
             dma((2,)), dma((2,)),
-            dma((2, 2)), dma((2, 2)), dma((2,)), dma((2,)),
+            dma((3, 4)), dma((3, 2)),
             dma((4,)), dma((4,)),
             dma((8,)), dma((8,)),
         ],

time: 126 us -> 124 us (0.984)
    unnamed x3 -> x1, local copies, waits for them, and re-layouts: 3.1 us -> 1.57 us
where the time goes in v4:
time: 124 us; the launch traced here: 123 us
  Pallas kernels  121 us (98%)
  local copies, waits for them, and re-layouts  2.15 us (2%)
    pallas_call x1, Pallas kernels, local(): pl.pallas_call(functools.partial(main_kernel, nz, nx, nl, cap, per_layer)...  121 us

profile of v4, /device:TPU:1, one launch (start us, length us, event | category | flops | bytes accessed | tf_op | source)
XLA Modules:
  0.0 123.5 jit_solution(8865941202789891020)
XLA Ops:
  0.0 0.7 pad_add_fusion
  0.7 0.6 pad.4
  1.3 120.6 %shard_map.46 = bf16[1,4,128,128]{3,2,1,0:T(8,128)(2,1)} custom-call(s32[4,1,128]{2,1,0:T(1,128)} %bitcast.7, bf16[96,128,128]{2,1,0:T(8,128)(2,1)} %bitcast.5, bf16[2,24,1,2,128,128]{5,4,3,2,1,0:T(8,128)(2,1)} %bitcast.6), custom_call_target="tpu_custom_call" | custom-call | tf_op jit(solution)/shard_map/pallas_call | solution.py:549
  121.9 1.6 %copy.6 = bf16[1,4,128,128]{3,2,1,0:T(8,128)(2,1)} copy(bf16[1,4,128,128]{3,2,1,0:T(8,128)(2,1)} %shard_map.46) | data formatting | bytes 262144

commit v5 on v4

--- a/solution.py
+++ b/solution.py
@@ -10,8 +10,8 @@
 MESH = pl.DeviceIdType.MESH
 SHIFT = 64
 CHUNK = 1
-PARTS = 3
-SPACING = 10
+PARTS = 6
+SPACING = 5
 HOP = 4
 LAG = 3
 PLANE_ROWS = 12

time: 124 us -> 124 us (level)
  no operation moved by 1% of the time
where the time goes in v5:
time: 124 us
  Pallas kernels  121 us (98%)
  local copies, waits for them, and re-layouts  2.15 us (2%)
    pallas_call x1, Pallas kernels, local(): pl.pallas_call(functools.partial(main_kernel, nz, nx, nl, cap, per_layer)...  121 us

profile of v5, /device:TPU:1, one launch (start us, length us, event | category | flops | bytes accessed | tf_op | source)
XLA Modules:
  0.0 124.2 jit_solution(6620379227623591975)
XLA Ops:
  0.0 0.7 pad_add_fusion
  0.7 0.6 pad.4
  1.3 121.4 %shard_map.46 = bf16[1,4,128,128]{3,2,1,0:T(8,128)(2,1)} custom-call(s32[4,1,128]{2,1,0:T(1,128)} %bitcast.7, bf16[96,128,128]{2,1,0:T(8,128)(2,1)} %bitcast.5, bf16[2,24,1,2,128,128]{5,4,3,2,1,0:T(8,128)(2,1)} %bitcast.6), custom_call_target="tpu_custom_call" | custom-call | tf_op jit(solution)/shard_map/pallas_call | solution.py:549
  122.7 1.6 %copy.6 = bf16[1,4,128,128]{3,2,1,0:T(8,128)(2,1)} copy(bf16[1,4,128,128]{3,2,1,0:T(8,128)(2,1)} %shard_map.46) | data formatting | bytes 262144
